TPU v7x, 256 devices: a whole 4x4x8 slice. The times are simulated.
256 devices in a mesh: dp: 16 (over x, z_lo), tm: 16 (over y, z_hi, core).
Axes of the slice: x: 4, y: 4, z: 8 (z_hi: 2, z_lo: 4; z = z_hi * 4 + z_lo), core: 2. Of those that a mesh axis runs over, the one named last changes fastest.
Arguments:
- frames: bfloat16 [16, 2048, 1536], P('dp', 'tm'), may hold values from -3 to 3
- query: bfloat16 [16, 2048, 1536], P('dp', 'tm'), may hold values from -6 to 6
- keys: bfloat16 [16, 2048, 1536], P('dp', 'tm'), may hold values from -6 to 6
- values: bfloat16 [16, 2048, 1536], P('dp', 'tm'), may hold values from -6 to 6
- norm_gain: float32 [1536], replicated, may hold values from 0.1 to 1.9
- conv_gain: float32 [1536], replicated, may hold values from 0.1 to 1.9
- w_glu: bfloat16 [1536, 3072], P('tm'), may hold values from -0.15625 to 0.15625
- taps: float32 [32, 1536], replicated, may hold values from -1 to 1
- w_out: bfloat16 [1536, 1536], P('tm'), may hold values from -0.15625 to 0.15625
- cotangent: bfloat16 [16, 2048, 1536], P('dp', 'tm'), may hold values from -0.03125 to 0.03125
Outputs:
- glu_grad: float32 [1536, 3072], P('tm')
- taps_grad: float32 [32, 1536], P(None, 'tm')
- out_grad: float32 [1536, 1536], P('tm')
All inputs are finite; a program needn't handle non-finite values.
Results may differ from a plain program's by a relative error of at most 0.02.
Values may be sent and summed in bfloat16 or wider, within the bound.
A program may use at most 128 MiB of HBM per device.

v0:
```python
import math

import jax
import jax.numpy as jnp
from jax import lax
from jax.sharding import PartitionSpec as P

HEADS = 16


def padded_2(value, sides, width):
    for axis, dim in sides:
        devices, length = (lax.axis_size(axis), value.shape[dim])
        up = [(i, (i + 1) % devices) for i in range(devices - 1)]
        down = [(j, i) for i, j in up]
        last = lax.slice_in_dim(value, length - width, length, axis=dim)
        leading = lax.slice_in_dim(value, 0, width, axis=dim)
        before = lax.ppermute(last, axis, up)
        after = lax.ppermute(leading, axis, down)
        value = jnp.concatenate([before, value, after], axis=dim)
    return value


def standard(v):
    mean = jnp.mean(v, axis=-1, keepdims=True)
    centred = v - mean
    var = jnp.mean(centred * centred, axis=-1, keepdims=True)
    inv = lax.rsqrt(var + 1e-05)
    return (centred * inv, inv)


def attend_heads(parts):
    q_all, k_all, v_all = parts
    length = q_all.shape[0]
    groups = q_all.shape[1]
    count = q_all.shape[2]
    head_dim = q_all.shape[3]
    q_flat = q_all.reshape(length, groups * count, head_dim)
    k_flat = k_all.reshape(length, groups * count, head_dim)
    v_flat = v_all.reshape(length, groups * count, head_dim)
    block = math.gcd(length, 512)
    scale = head_dim ** (-0.5)
    q_blocks = q_flat.reshape(length // block, block, groups * count, head_dim)

    def one_block(q_part):
        scores = (
            jnp.einsum("qhd,khd->hqk", q_part, k_flat, preferred_element_type=jnp.float32) * scale
        )
        top = jnp.max(scores, axis=2, keepdims=True)
        expo = jnp.exp(scores - top)
        total = jnp.sum(expo, axis=2)
        weights = expo.astype(jnp.bfloat16)
        summed = jnp.einsum("hqk,khd->qhd", weights, v_flat, preferred_element_type=jnp.float32)
        return (summed / total.T[:, :, None]).astype(jnp.bfloat16)

    return lax.map(one_block, q_blocks).reshape(length, groups, count, head_dim)


def add_rows(left, piece):
    return jnp.dot(left, piece, preferred_element_type=jnp.float32)


def project_back(cot_rows, piece):
    return lax.dot_general(
        cot_rows, piece, (((1,), (1,)), ((), ())), preferred_element_type=jnp.float32
    )


def rim_rows(field, half):
    return padded_2(field, (("tm", 0),), half)


def row_product(left, right):
    return lax.dot_general(
        left, right, (((0,), (0,)), ((), ())), preferred_element_type=jnp.float32
    )


def local(frames, query, keys, values, norm_gain, conv_gain, w_glu, taps, w_out, cotangent):
    rows = frames.shape[1]
    width = frames.shape[2]
    head_dim = width // HEADS
    groups = lax.axis_size("tm")
    per_group = HEADS // groups
    kernel = taps.shape[0]
    half = kernel // 2

    def split_heads(arr):
        return arr[0].reshape(rows, groups, per_group, head_dim)

    heads_out = attend_heads(
        (
            lax.all_to_all(split_heads(query), "tm", split_axis=1, concat_axis=0, tiled=True),
            lax.all_to_all(split_heads(keys), "tm", split_axis=1, concat_axis=0, tiled=True),
            lax.all_to_all(split_heads(values), "tm", split_axis=1, concat_axis=0, tiled=True),
        )
    )
    attention = lax.all_to_all(heads_out, "tm", split_axis=0, concat_axis=1, tiled=True).reshape(
        rows, width
    )
    mixed = frames[0].astype(jnp.float32) + attention.astype(jnp.float32)
    normed, unused = standard(mixed)
    u_rows = (normed * norm_gain).astype(jnp.bfloat16)
    p_full = add_rows(u_rows, lax.all_gather(w_glu, "tm", axis=0, tiled=True))
    first = p_full[:, :width]
    sig = jax.nn.sigmoid(p_full[:, width:])
    y_rows = (first * sig).astype(jnp.bfloat16)
    padded = rim_rows(y_rows, half)
    z_rows = jnp.zeros((rows, width), jnp.float32)
    for k in range(kernel):
        z_rows = z_rows + taps[k] * padded[k : k + rows].astype(jnp.float32)
    zhat, inv = standard(z_rows)
    n_rows = zhat * conv_gain
    sgate = jax.nn.sigmoid(n_rows)
    s_rows = (n_rows * sgate).astype(jnp.bfloat16)
    cot_rows = cotangent[0]
    d_s = project_back(cot_rows, lax.all_gather(w_out, "tm", axis=0, tiled=True))
    d_n = d_s * sgate * (1.0 + n_rows * (1.0 - sgate))
    e_rows = d_n * conv_gain
    d_z = (
        (
            e_rows
            - jnp.mean(e_rows, axis=-1, keepdims=True)
            - zhat * jnp.mean(e_rows * zhat, axis=-1, keepdims=True)
        )
        * inv
    ).astype(jnp.bfloat16)
    dz_pad = rim_rows(d_z, half)
    d_y = jnp.zeros((rows, width), jnp.float32)
    for k in range(kernel):
        d_y = d_y + taps[k] * dz_pad[2 * half - k : 2 * half - k + rows].astype(jnp.float32)
    d_p = jnp.concatenate([d_y * sig, d_y * first * sig * (1.0 - sig)], axis=1).astype(jnp.bfloat16)
    dz_float = d_z.astype(jnp.float32)
    taps_term = jnp.stack(
        [
            jnp.sum(dz_float * padded[k : k + rows].astype(jnp.float32), axis=0)
            for k in range(kernel)
        ]
    )
    glu_term = row_product(u_rows, d_p)
    glu_share, taps_share, out_share = (
        lax.psum_scatter(
            glu_term.astype(jnp.bfloat16), "tm", scatter_dimension=0, tiled=True
        ).astype(jnp.float32),
        lax.psum_scatter(
            taps_term.astype(jnp.bfloat16), "tm", scatter_dimension=1, tiled=True
        ).astype(jnp.float32),
        lax.psum_scatter(
            row_product(s_rows, cot_rows).astype(jnp.bfloat16),
            "tm",
            scatter_dimension=0,
            tiled=True,
        ).astype(jnp.float32),
    )
    glu_grad, taps_grad, out_grad = (
        lax.psum(glu_share.astype(jnp.bfloat16), "dp").astype(jnp.float32),
        lax.psum(taps_share.astype(jnp.bfloat16), "dp").astype(jnp.float32),
        lax.psum(out_share.astype(jnp.bfloat16), "dp").astype(jnp.float32),
    )
    return (glu_grad, taps_grad, out_grad)


def solution(mesh):
    return jax.shard_map(
        local,
        mesh=mesh,
        in_specs=(
            P("dp", "tm", None),
            P("dp", "tm", None),
            P("dp", "tm", None),
            P("dp", "tm", None),
            P(),
            P(),
            P("tm", None),
            P(),
            P("tm", None),
            P("dp", "tm", None),
        ),
        out_specs=(P("tm", None), P(None, "tm"), P("tm", None)),
        check_vma=False,
    )
```

profile of v0, /device:TPU:1, one launch (start us, length us, event | category | flops | bytes accessed | tf_op | source)
XLA Modules:
  0.0 724.8 jit_solution(1451426900829549947)
XLA Ops:
  7.9 1.9 copy.42
  9.8 12.6 %all-to-all-start = ((bf16[128,16,1,96]{0,3,2,1:T(8,128)(2,1)}), bf16[128,16,1,96]{0,3,2,1:T(8,128)(2,1)S(1)}, u32[]{:S(2)}, u32[]{:S(2)}) async-start(bf16[128,16,1,96]{0,3,2,1:T(8,128)(2,1)} %bitcast.9), calls=%async_computation | async-start | bytes 786432 | tf_op jit(solution)/shard_map/all_to_all | solution.py:93
  22.4 1.9 copy.45
  24.4 10.6 %all-to-all-done = bf16[128,16,1,96]{0,3,2,1:T(8,128)(2,1)S(1)} async-done(((bf16[128,16,1,96]{0,3,2,1:T(8,128)(2,1)}), bf16[128,16,1,96]{0,3,2,1:T(8,128)(2,1)S(1)}, u32[]{:S(2)}, u32[]{:S(2)}) %all-to-all-start) | async-done | bytes 393248 | tf_op jit(solution)/shard_map/all_to_all | solution.py:93
  34.9 5.5 all-to-all-start.1
  40.5 1.9 copy.48
  42.4 13.5 %all-to-all-done.1 = bf16[128,16,1,96]{0,3,2,1:T(8,128)(2,1)S(1)} async-done(((bf16[128,16,1,96]{0,3,2,1:T(8,128)(2,1)}), bf16[128,16,1,96]{0,3,2,1:T(8,128)(2,1)S(1)}, u32[]{:S(2)}, u32[]{:S(2)}) %all-to-all-start.1) | async-done | bytes 393248 | tf_op jit(solution)/shard_map/all_to_all | solution.py:94
  55.9 7.0 all-to-all-start.2
  64.4 12.4 %all-to-all-done.2 = bf16[128,16,1,96]{0,3,2,1:T(8,128)(2,1)S(1)} async-done(((bf16[128,16,1,96]{0,3,2,1:T(8,128)(2,1)}), bf16[128,16,1,96]{0,3,2,1:T(8,128)(2,1)S(1)}, u32[]{:S(2)}, u32[]{:S(2)}) %all-to-all-start.2) | async-done | bytes 393248 | tf_op jit(solution)/shard_map/all_to_all | solution.py:95
  77.1 10.5 %while.10 = (s32[]{:T(128)}, bf16[4,512,1,96]{1,3,2,0:T(8,128)(2,1)S(1)}, bf16[4,512,1,96]{1,3,2,0:T(8,128)(2,1)S(1)}, bf16[2048,1,96]{0,2,1:T(8,128)(2,1)S(1)}, bf16[2048,1,96]{0,2,1:T(8,128)(2,1)S(1)}, /*index=5*/s32[]{:T(128)}) while((s32[]{:T(128)}, bf16[4,512,1,96]{1,3,2,0:T(8,128)(2,1)S(1)}, bf16[4,512,1,96]{1,3,2,0:T(8,128)(2,1)S(1)}, ...), condition=%wide.region_3.4_spmd, body=%wide.region_0.3_spmd.sunk | while | flops 411139072 | bytes 13576269 | solution.py:56
  78.0 0.8 fusion.197
  78.8 1.0 fusion.198
  80.6 0.8 fusion.197
  81.4 1.0 fusion.198
  83.2 0.8 fusion.197
  84.0 1.0 fusion.198
  85.8 0.8 fusion.197
  86.6 1.0 fusion.198
  88.7 11.5 %reduce.68 = bf16[2048,96]{1,0:T(8,128)(2,1)S(1)} reduce(bf16[2048,1,1,96]{3,2,1,0:T(2,128)(2,1)S(1)} %reshape.94, bf16[]{:T(256)} %broadcast.137), dimensions={1,2}, to_apply=%reshape.94.reduce_sub_computation | reduce | bytes 786434 | tf_op jit(solution)/shard_map/reshape | solution.py:56
  100.2 1.6 reshape.129
  101.8 5.5 all-to-all-start.3
  107.8 0.9 slice_reduce_fusion.31
  108.7 26.2 %all-to-all-done.3 = bf16[16,2,6144]{2,1,0:T(2,128)(2,1)S(1)} async-done(((bf16[16,2,6144]{2,1,0:T(2,128)(2,1)}), bf16[16,2,6144]{2,1,0:T(2,128)(2,1)S(1)}, u32[]{:S(2)}, u32[]{:S(2)}) %all-to-all-start.3) | async-done | bytes 393248 | tf_op jit(solution)/shard_map/all_to_all | solution.py:98
  137.6 1.9 all-gather.5.cloned.1.call-done
  139.7 5.2 fusion.186
  145.1 4.7 collective-permute-start
  149.8 1.9 collective-permute-start.1
  152.1 7.0 collective-permute-done.1
  159.3 4.1 fusion.182
  163.7 3.8 convolution_convert_fusion.1
  167.5 55.5 %all-gather.3.cloned.1.call-done = bf16[1536,1536]{1,0:T(8,128)(2,1)} async-done(((bf16[96,1536]{1,0:T(8,128)(2,1)}), bf16[1536,1536]{1,0:T(8,128)(2,1)}) %all-gather.3.cloned.1.call-update) | async-done | bytes 4718608 | tf_op jit(solution)/shard_map/all_gather | solution.py:117
  223.1 4.1 fusion.180
  227.4 4.4 fusion.106
  231.7 2.2 collective-permute-start.2
  233.9 7.5 %collective-permute-start.3 = (bf16[16,1536]{1,0:T(8,128)(2,1)S(1)}, bf16[16,1536]{1,0:T(8,128)(2,1)S(1)}, u32[]{:S(2)}, u32[]{:S(2)}) collective-permute-start(bf16[16,1536]{1,0:T(8,128)(2,1)S(1)} %get-tuple-element.132), channel_id=1, source_target_pairs={{0,1},{1,2},{2,3},{3,4},{4,5},{5,6},{6,7},{7,8},{8,9},{9,10},{10,1... | collective-permute-start | bytes 147464 | tf_op jit(solution)/shard_map/ppermute | solution.py:18
  241.4 0.9 collective-permute-done.3
  242.3 5.5 multiply_convert_fusion.2
  248.2 5.2 convolution_convert_fusion
  255.1 1.1 fusion.90
  256.3 0.8 fusion.89
  257.8 0.9 copy.57
  258.8 70.8 %reduce-scatter.8.cloned.1.call-done = bf16[96,1536]{1,0:T(8,128)(2,1)} async-done(((bf16[1536,1536]{1,0:T(8,128)(2,1)}), bf16[96,1536]{1,0:T(8,128)(2,1)}) %reduce-scatter.8.cloned.1.call-update) | async-done | bytes 294928 | tf_op jit(solution)/shard_map/reduce_scatter | solution.py:148
  329.6 152.9 %reduce-scatter.6.cloned.1.call-done = bf16[96,3072]{1,0:T(8,128)(2,1)} async-done(((bf16[1536,3072]{1,0:T(8,128)(2,1)}), bf16[96,3072]{1,0:T(8,128)(2,1)}) %reduce-scatter.6.cloned.1.call-update) | async-done | bytes 589840 | tf_op jit(solution)/shard_map/reduce_scatter | solution.py:142
  482.5 76.2 %reduce-scatter.10.cloned.1.call-done = bf16[96,32]{1,0:T(8,128)(2,1)} async-done(((bf16[1536,32]{1,0:T(8,128)(2,1)}), bf16[96,32]{1,0:T(8,128)(2,1)}) %reduce-scatter.10.cloned.1.call-update) | async-done | bytes 6160
  559.5 35.8 %psum.22 = bf16[32,96]{1,0:T(8,128)(2,1)S(1)} all-reduce(bf16[32,96]{1,0:T(8,128)(2,1)S(1)} %copy.58), channel_id=1, replica_groups=mesh['dp'=16,'tm'=16] {'dp'}, use_global_device_ids=true, to_apply=%region_45.46 | all-reduce | flops 3072 | bytes 12288 | tf_op jit(solution)/shard_map/psum | solution.py:157
  595.9 118.1 %all-reduce.3.cloned.1.call-done = (bf16[96,3072]{1,0:T(8,128)(2,1)}, bf16[96,1536]{1,0:T(8,128)(2,1)}) async-done(((bf16[96,3072]{1,0:T(8,128)(2,1)}, bf16[96,1536]{1,0:T(8,128)(2,1)}), (bf16[96,3072]{1,0:T(8,128)(2,1)}, bf16[96,1536]{1,0:T(8,128)(2,1)})) %all-reduce.3.cloned.1.call-update) | async-done | bytes 884752 | tf_op jit(solution)/shard_map/psum | solution.py:156
  714.0 2.2 convert_element_type.362
  716.1 1.8 convert_element_type.366
  (187 shorter events, 14.7 us)
Async XLA Ops:
  7.2 156.5 %copy-start = (bf16[1,128,1536]{2,1,0:T(8,128)(2,1)S(1)}, bf16[1,128,1536]{2,1,0:T(8,128)(2,1)}, u32[]{:S(2)}) copy-start(bf16[1,128,1536]{2,1,0:T(8,128)(2,1)} %param.21) | copy-start | bytes 1179652
  7.2 132.3 %all-gather.5.cloned.1.call-start = ((), (), s32[]{:S(2)}) async-start(), calls=%async_computation.8 | async-start | bytes 10027008 | tf_op jit(solution)/shard_map/all_gather | solution.py:104
  9.8 25.1 %all-to-all-start = ((bf16[128,16,1,96]{0,3,2,1:T(8,128)(2,1)}), bf16[128,16,1,96]{0,3,2,1:T(8,128)(2,1)S(1)}, u32[]{:S(2)}, u32[]{:S(2)}) async-start(bf16[128,16,1,96]{0,3,2,1:T(8,128)(2,1)} %bitcast.9), calls=%async_computation | async-start | bytes 786432 | tf_op jit(solution)/shard_map/all_to_all | solution.py:93
  34.9 21.0 %all-to-all-start.1 = ((bf16[128,16,1,96]{0,3,2,1:T(8,128)(2,1)}), bf16[128,16,1,96]{0,3,2,1:T(8,128)(2,1)S(1)}, u32[]{:S(2)}, u32[]{:S(2)}) async-start(bf16[128,16,1,96]{0,3,2,1:T(8,128)(2,1)} %bitcast.13), calls=%async_computation.1 | async-start | bytes 786432 | tf_op jit(solution)/shard_map/all_to_all | solution.py:94
  55.9 20.9 %all-to-all-start.2 = ((bf16[128,16,1,96]{0,3,2,1:T(8,128)(2,1)}), bf16[128,16,1,96]{0,3,2,1:T(8,128)(2,1)S(1)}, u32[]{:S(2)}, u32[]{:S(2)}) async-start(bf16[128,16,1,96]{0,3,2,1:T(8,128)(2,1)} %bitcast.17), calls=%async_computation.2 | async-start | bytes 786432 | tf_op jit(solution)/shard_map/all_to_all | solution.py:95
  62.9 160.2 %all-gather.3.cloned.1.call-start = ((), (), s32[]{:S(2)}) async-start(), calls=%async_computation.7 | async-start | bytes 5013504 | tf_op jit(solution)/shard_map/all_gather | solution.py:117
  87.6 19.9 %copy-start.7 = (bf16[1,128,1536]{2,1,0:T(8,128)(2,1)S(1)}, bf16[1,128,1536]{2,1,0:T(8,128)(2,1)}, u32[]{:S(2)}) copy-start(bf16[1,128,1536]{2,1,0:T(8,128)(2,1)} %param.12) | copy-start | bytes 1179652
  87.6 20.1 %copy-start.8 = (f32[32,1536]{1,0:T(8,128)S(1)}, f32[32,1536]{1,0:T(8,128)}, u32[]{:S(2)}) copy-start(f32[32,1536]{1,0:T(8,128)} %param.19) | copy-start | bytes 589828
  101.8 33.1 %all-to-all-start.3 = ((bf16[16,2,6144]{2,1,0:T(2,128)(2,1)}), bf16[16,2,6144]{2,1,0:T(2,128)(2,1)S(1)}, u32[]{:S(2)}, u32[]{:S(2)}) async-start(bf16[16,2,6144]{2,1,0:T(2,128)(2,1)} %reshape.129), calls=%async_computation.3 | async-start | bytes 786432 | tf_op jit(solution)/shard_map/all_to_all | solution.py:98
  107.3 222.3 %reduce-scatter.8.cloned.1.call-start = ((), (), s32[]{:S(2)}) async-start(), calls=%async_computation.10 | async-start | bytes 5013504 | tf_op jit(solution)/shard_map/reduce_scatter | solution.py:148
  139.5 19.6 %copy-start.12 = (f32[1536]{0:T(1024)S(1)}, f32[1536]{0:T(1024)}, u32[]{:S(2)}) copy-start(f32[1536]{0:T(1024)} %get-tuple-element.83) | copy-start | bytes 18436
  139.5 19.6 %copy-start.13 = (f32[1536]{0:T(1024)S(1)}, f32[1536]{0:T(1024)}, u32[]{:S(2)}) copy-start(f32[1536]{0:T(1024)} %get-tuple-element.84) | copy-start | bytes 18436
  139.5 19.6 %copy-start.14 = (f32[1536]{0:T(1024)S(1)}, f32[1536]{0:T(1024)}, u32[]{:S(2)}) copy-start(f32[1536]{0:T(1024)} %get-tuple-element.85) | copy-start | bytes 18436
  139.5 19.6 %copy-start.15 = (f32[1536]{0:T(1024)S(1)}, f32[1536]{0:T(1024)}, u32[]{:S(2)}) copy-start(f32[1536]{0:T(1024)} %get-tuple-element.86) | copy-start | bytes 18436
  139.5 19.6 %copy-start.16 = (f32[1536]{0:T(1024)S(1)}, f32[1536]{0:T(1024)}, u32[]{:S(2)}) copy-start(f32[1536]{0:T(1024)} %get-tuple-element.87) | copy-start | bytes 18436
  139.6 19.6 %copy-start.17 = (f32[1536]{0:T(1024)S(1)}, f32[1536]{0:T(1024)}, u32[]{:S(2)}) copy-start(f32[1536]{0:T(1024)} %get-tuple-element.88) | copy-start | bytes 18436
  139.6 19.6 %copy-start.18 = (f32[1536]{0:T(1024)S(1)}, f32[1536]{0:T(1024)}, u32[]{:S(2)}) copy-start(f32[1536]{0:T(1024)} %get-tuple-element.89) | copy-start | bytes 18436
  139.6 19.6 %copy-start.19 = (f32[1536]{0:T(1024)S(1)}, f32[1536]{0:T(1024)}, u32[]{:S(2)}) copy-start(f32[1536]{0:T(1024)} %get-tuple-element.90) | copy-start | bytes 18436
  139.6 19.6 %copy-start.20 = (f32[1536]{0:T(1024)S(1)}, f32[1536]{0:T(1024)}, u32[]{:S(2)}) copy-start(f32[1536]{0:T(1024)} %get-tuple-element.91) | copy-start | bytes 18436
  139.6 19.6 %copy-start.21 = (f32[1536]{0:T(1024)S(1)}, f32[1536]{0:T(1024)}, u32[]{:S(2)}) copy-start(f32[1536]{0:T(1024)} %get-tuple-element.92) | copy-start | bytes 18436
  139.6 19.6 %copy-start.22 = (f32[1536]{0:T(1024)S(1)}, f32[1536]{0:T(1024)}, u32[]{:S(2)}) copy-start(f32[1536]{0:T(1024)} %get-tuple-element.93) | copy-start | bytes 18436
  139.6 19.6 %copy-start.23 = (f32[1536]{0:T(1024)S(1)}, f32[1536]{0:T(1024)}, u32[]{:S(2)}) copy-start(f32[1536]{0:T(1024)} %get-tuple-element.94) | copy-start | bytes 18436
  139.6 19.6 %copy-start.24 = (f32[1536]{0:T(1024)S(1)}, f32[1536]{0:T(1024)}, u32[]{:S(2)}) copy-start(f32[1536]{0:T(1024)} %get-tuple-element.95) | copy-start | bytes 18436
  139.6 19.6 %copy-start.25 = (f32[1536]{0:T(1024)S(1)}, f32[1536]{0:T(1024)}, u32[]{:S(2)}) copy-start(f32[1536]{0:T(1024)} %get-tuple-element.96) | copy-start | bytes 18436
  139.6 19.6 %copy-start.26 = (f32[1536]{0:T(1024)S(1)}, f32[1536]{0:T(1024)}, u32[]{:S(2)}) copy-start(f32[1536]{0:T(1024)} %get-tuple-element.97) | copy-start | bytes 18436
  139.7 19.6 %copy-start.27 = (f32[1536]{0:T(1024)S(1)}, f32[1536]{0:T(1024)}, u32[]{:S(2)}) copy-start(f32[1536]{0:T(1024)} %get-tuple-element.98) | copy-start | bytes 18436
  145.1 7.0 collective-permute-start
  149.8 9.3 %collective-permute-start.1 = (bf16[16,1536]{1,0:T(8,128)(2,1)S(1)}, bf16[16,1536]{1,0:T(8,128)(2,1)S(1)}, u32[]{:S(2)}, u32[]{:S(2)}) collective-permute-start(bf16[16,1536]{1,0:T(8,128)(2,1)S(1)} %get-tuple-element.134), channel_id=1, source_target_pairs={{1,0},{2,1},{3,2},{4,3},{5,4},{6,5},{7,6},{8,7},{9,8},{10,9},{11,1... | collective-permute-start | bytes 147464 | tf_op jit(solution)/shard_map/ppermute | solution.py:19
  152.0 75.3 %copy-start.29 = (f32[1536]{0:T(1024)}, f32[1536]{0:T(1024)S(1)}, u32[]{:S(2)}) copy-start(f32[1536]{0:T(1024)S(1)} %get-tuple-element.100) | copy-start | bytes 18436
  152.0 75.3 %copy-start.30 = (f32[1536]{0:T(1024)}, f32[1536]{0:T(1024)S(1)}, u32[]{:S(2)}) copy-start(f32[1536]{0:T(1024)S(1)} %get-tuple-element.101) | copy-start | bytes 18436
  152.0 75.3 %copy-start.31 = (f32[1536]{0:T(1024)}, f32[1536]{0:T(1024)S(1)}, u32[]{:S(2)}) copy-start(f32[1536]{0:T(1024)S(1)} %get-tuple-element.102) | copy-start | bytes 18436
  152.0 75.3 %copy-start.32 = (f32[1536]{0:T(1024)}, f32[1536]{0:T(1024)S(1)}, u32[]{:S(2)}) copy-start(f32[1536]{0:T(1024)S(1)} %get-tuple-element.103) | copy-start | bytes 18436
  152.0 75.3 %copy-start.33 = (f32[1536]{0:T(1024)}, f32[1536]{0:T(1024)S(1)}, u32[]{:S(2)}) copy-start(f32[1536]{0:T(1024)S(1)} %get-tuple-element.104) | copy-start | bytes 18436
  152.0 75.3 %copy-start.34 = (f32[1536]{0:T(1024)}, f32[1536]{0:T(1024)S(1)}, u32[]{:S(2)}) copy-start(f32[1536]{0:T(1024)S(1)} %get-tuple-element.105) | copy-start | bytes 18436
  152.0 75.3 %copy-start.35 = (f32[1536]{0:T(1024)}, f32[1536]{0:T(1024)S(1)}, u32[]{:S(2)}) copy-start(f32[1536]{0:T(1024)S(1)} %get-tuple-element.106) | copy-start | bytes 18436
  152.0 75.3 %copy-start.36 = (f32[1536]{0:T(1024)}, f32[1536]{0:T(1024)S(1)}, u32[]{:S(2)}) copy-start(f32[1536]{0:T(1024)S(1)} %get-tuple-element.107) | copy-start | bytes 18436
  152.0 75.3 %copy-start.37 = (f32[1536]{0:T(1024)}, f32[1536]{0:T(1024)S(1)}, u32[]{:S(2)}) copy-start(f32[1536]{0:T(1024)S(1)} %get-tuple-element.108) | copy-start | bytes 18436
  152.1 75.3 %copy-start.38 = (f32[1536]{0:T(1024)}, f32[1536]{0:T(1024)S(1)}, u32[]{:S(2)}) copy-start(f32[1536]{0:T(1024)S(1)} %get-tuple-element.109) | copy-start | bytes 18436
  152.1 75.3 %copy-start.39 = (f32[1536]{0:T(1024)}, f32[1536]{0:T(1024)S(1)}, u32[]{:S(2)}) copy-start(f32[1536]{0:T(1024)S(1)} %get-tuple-element.110) | copy-start | bytes 18436
  152.1 75.3 %copy-start.40 = (f32[1536]{0:T(1024)}, f32[1536]{0:T(1024)S(1)}, u32[]{:S(2)}) copy-start(f32[1536]{0:T(1024)S(1)} %get-tuple-element.111) | copy-start | bytes 18436
  163.4 59.7 %copy-start.49 = (f32[128]{0:T(128)}, f32[128]{0:T(128)S(1)}, u32[]{:S(2)}) copy-start(f32[128]{0:T(128)S(1)} %broadcast_multiply_fusion.2) | copy-start | bytes 1540
  163.7 59.4 %copy-start.50 = (f32[128]{0:T(128)}, f32[128]{0:T(128)S(1)}, u32[]{:S(2)}) copy-start(f32[128]{0:T(128)S(1)} %add_rsqrt_fusion) | copy-start | bytes 1540
  167.5 315.0 %reduce-scatter.6.cloned.1.call-start = ((), (), s32[]{:S(2)}) async-start(), calls=%async_computation.9 | async-start | bytes 10027008 | tf_op jit(solution)/shard_map/reduce_scatter | solution.py:142
  227.3 20.8 %copy-start.2 = (bf16[128,1536]{0,1:T(8,128)(2,1)S(1)}, bf16[128,1536]{0,1:T(8,128)(2,1)}, u32[]{:S(2)}) copy-start(bf16[128,1536]{0,1:T(8,128)(2,1)} %copy-done.1) | copy-start | bytes 1179652
  231.7 9.7 %collective-permute-start.2 = (bf16[16,1536]{1,0:T(8,128)(2,1)S(1)}, bf16[16,1536]{1,0:T(8,128)(2,1)S(1)}, u32[]{:S(2)}, u32[]{:S(2)}) collective-permute-start(bf16[16,1536]{1,0:T(8,128)(2,1)S(1)} %get-tuple-element.131), channel_id=1, source_target_pairs={{1,0},{2,1},{3,2},{4,3},{5,4},{6,5},{7,6},{8,7},{9,8},{10,9},{11,1... | collective-permute-start | bytes 147464 | tf_op jit(solution)/shard_map/ppermute | solution.py:19
  233.9 8.5 %collective-permute-start.3 = (bf16[16,1536]{1,0:T(8,128)(2,1)S(1)}, bf16[16,1536]{1,0:T(8,128)(2,1)S(1)}, u32[]{:S(2)}, u32[]{:S(2)}) collective-permute-start(bf16[16,1536]{1,0:T(8,128)(2,1)S(1)} %get-tuple-element.132), channel_id=1, source_target_pairs={{0,1},{1,2},{2,3},{3,4},{4,5},{5,6},{6,7},{7,8},{8,9},{9,10},{10,1... | collective-permute-start | bytes 147464 | tf_op jit(solution)/shard_map/ppermute | solution.py:18
  253.4 305.3 %reduce-scatter.10.cloned.1.call-start = ((), (), s32[]{:S(2)}) async-start(), calls=%async_computation.11 | async-start | bytes 417792
  258.7 455.2 %all-reduce.3.cloned.1.call-start = ((), (), s32[]{:S(2)}) async-start(), calls=%async_computation.12 | async-start | bytes 1769472 | tf_op jit(solution)/shard_map/psum | solution.py:156
  (17 other events, 128.1 us)
Sparse Core Ops, SparseCore 0:
  10.7 128.7 all-gather.4
  142.2 80.7 all-gather.2
  227.4 102.1 reduce-scatter.7
  334.9 147.5 reduce-scatter.5
  487.4 71.2 reduce-scatter.9
  561.4 152.4 all-reduce.2
where the time goes:
time: 735 us; the launch traced here: 725 us
  waiting for transfers between devices  548 us (75%)
  starting transfers between devices  47.3 us (6%)
  other arithmetic  37.7 us (5%)
  blocking collectives  35.8 us (5%)
  matrix products  25.4 us (3%)
  local copies, waits for them, and re-layouts  15.7 us (2%)
  between operations  15.3 us (2%)
    reduce_scatter x1, waiting for transfers between devices, local(): lax.psum_scatter(glu_term.astype(jnp.bfloat16), 'tm', scatter_dimension=0...  153 us
    psum x1, waiting for transfers between devices, local(): lax.psum(glu_share.astype(jnp.bfloat16), 'dp').astype(jnp.float32)  118 us
    unnamed x7, waiting for transfers between devices  77.6 us
    reduce_scatter x1, waiting for transfers between devices, local(): lax.psum_scatter(row_product(s_rows, cot_rows).astype(jnp.bfloat16), 'tm'...  70.8 us
    all_gather x1, waiting for transfers between devices, local(): lax.all_gather(w_out, 'tm', axis=0, tiled=True)  55.5 us
    psum x1, blocking collectives, local(): lax.psum(taps_share.astype(jnp.bfloat16), 'dp').astype(jnp.float32)  35.8 us
    all_to_all x1, waiting for transfers between devices, local(): lax.all_to_all(heads_out, 'tm', split_axis=0, concat_axis=1, tiled=True)  26.2 us
  transfers between devices with their start and end apart: 14, of which 12 were waited for; matrix products, arithmetic and copies ran while one was open for 10% of the time, Pallas kernels for 0%

commit v1 on v0

v1 whole, which is shorter than its diff:
```python
import functools

import jax
import jax.numpy as jnp
from jax import lax
from jax.experimental import pallas as pl
from jax.experimental.pallas import tpu as pltpu
from jax.sharding import PartitionSpec as P

N = 16
HD = 96
MESH = pl.DeviceIdType.MESH
F32 = jnp.float32
BF16 = jnp.bfloat16
EPS = 1e-05
TAIL = 16


def rem_copy(src, dst, send, recv, peer):
    return pltpu.make_async_remote_copy(
        src_ref=src, dst_ref=dst, send_sem=send, recv_sem=recv, device_id=peer, device_id_type=MESH
    )


def tm_barrier(me):
    barrier = pltpu.get_barrier_semaphore()
    for i in range(1, N):
        pl.semaphore_signal(
            barrier, inc=1, device_id={"tm": lax.rem(me + i, N)}, device_id_type=MESH
        )
    pl.semaphore_wait(barrier, N - 1)


class Gather:
    def __init__(self, me, own, out, send, recv, local):
        self.own, self.out, self.send, self.recv, self.local = own, out, send, recv, local
        y = me // 4
        z = lax.rem(me // 2, 2)
        c = lax.rem(me, 2)
        at = lambda yy, zz, cc: lax.rem(yy, 4) * 4 + zz * 2 + cc
        self.me = me
        self.far = at(y, 1 - z, c)
        self.sib = at(y, z, 1 - c)
        self.to = [at(y + j, z, c) for j in range(1, 4)]
        self.frm = [at(y + 4 - j, z, c) for j in range(1, 4)]
        self.frm_far = [at(y + 4 - j, 1 - z, c) for j in range(1, 4)]
        self.frm_sib = (
            [self.sib, at(y, 1 - z, 1 - c)]
            + [at(y + 4 - j, z, 1 - c) for j in range(1, 4)]
            + [at(y + 4 - j, 1 - z, 1 - c) for j in range(1, 4)]
        )
        self.started = []

    def go(self, src, slot, sem, peer):
        copy = rem_copy(
            src, self.out.at[slot], self.send.at[sem], self.recv.at[sem], {"tm": peer}
        )
        copy.start()
        self.started.append(copy)

    def landed(self, slot, sem):
        ref = self.out.at[slot]
        rem_copy(ref, ref, self.send.at[sem], self.recv.at[sem], {"tm": self.sib}).wait_recv()

    def start(self):
        self.keep = pltpu.make_async_copy(self.own, self.out.at[self.me], self.local)
        self.go(self.own, self.me, 0, self.far)
        for j in range(3):
            self.go(self.own, self.me, 1 + j, self.to[j])
        self.go(self.own, self.me, 7, self.sib)
        self.keep.start()

    def relay_far(self):
        self.landed(self.far, 0)
        for j in range(3):
            self.go(self.out.at[self.far], self.far, 4 + j, self.to[j])
        self.go(self.out.at[self.far], self.far, 8, self.sib)

    def relay_near(self):
        for j in (0, 2, 1):
            self.landed(self.frm[j], 1 + j)
            self.go(self.out.at[self.frm[j]], self.frm[j], 9 + j, self.sib)

    def relay_rest(self):
        for j in (0, 2, 1):
            self.landed(self.frm_far[j], 4 + j)
            self.go(self.out.at[self.frm_far[j]], self.frm_far[j], 12 + j, self.sib)

    def finish(self):
        for k in range(8):
            self.landed(self.frm_sib[k], 7 + k)
        for copy in self.started:
            copy.wait_send()
        self.keep.wait()


class Swap:
    def __init__(self, me, buf, send, recv):
        self.me, self.buf, self.send, self.recv = me, buf, send, recv
        self.started = []

    def start(self):
        for i in range(1, N):
            copy = rem_copy(
                self.buf.at[self.me],
                self.buf.at[self.me],
                self.send.at[i],
                self.recv.at[i],
                {"tm": lax.rem(self.me + i, N)},
            )
            copy.start()
            self.started.append(copy)

    def finish(self):
        for i in range(1, N):
            ref = self.buf.at[lax.rem(self.me + N - i, N)]
            rem_copy(ref, ref, self.send.at[i], self.recv.at[i], {"tm": self.me}).wait_recv()
        for copy in self.started:
            copy.wait_send()


def own_stats(x):
    mean = jnp.mean(x, axis=0, keepdims=True)
    dev = x - mean
    return mean, jnp.sum(dev * dev, axis=0, keepdims=True)


def joined_stats(buf):
    means = buf[:, 0, :]
    squares = buf[:, 1, :]
    mean = jnp.mean(means, axis=0, keepdims=True)
    dev = means - mean
    total = jnp.sum(squares, axis=0, keepdims=True) + HD * jnp.sum(dev * dev, axis=0, keepdims=True)
    return mean, lax.rsqrt(total * (1.0 / (N * HD)) + EPS)


def front_kernel(
    q_ref, k_ref, v_ref, f_ref, w_ref, cot_ref, gain_ref,
    u_out, cot_out, w_out,
    packed, got, k_rows, v_cols, mixed, stats, own_u,
    x_send, x_recv, w_send, w_recv, s_send, s_recv, c_send, c_recv, u_send, u_recv, keep_sem,
):
    me = lax.axis_index("tm")
    length = mixed.shape[1]
    rows = q_ref.shape[0]
    for a, ref in enumerate((k_ref, v_ref, q_ref, f_ref)):
        turned = jnp.transpose(ref[...])
        for d in range(N):
            packed[d, a * HD : (a + 1) * HD, :] = turned[d * HD : (d + 1) * HD]
    tm_barrier(me)
    cot = Gather(me, cot_ref, cot_out, c_send, c_recv, keep_sem.at[0])
    x_copies, w_copies = [], []
    for i in range(1, N):
        peer = lax.rem(me + i, N)
        copy = rem_copy(packed.at[peer], got.at[me], x_send.at[i], x_recv.at[i], {"tm": peer})
        copy.start()
        x_copies.append(copy)
    cot.start()
    for i in range(1, N):
        peer = lax.rem(me + i, N)
        copy = rem_copy(w_ref.at[peer], w_out.at[me], w_send.at[i], w_recv.at[i], {"tm": peer})
        copy.start()
        w_copies.append(copy)
    w_keep = pltpu.make_async_copy(w_ref.at[me], w_out.at[me], keep_sem.at[1])
    w_keep.start()
    got[me] = packed[me]
    for i in range(1, N):
        ref = got.at[lax.rem(me + N - i, N)]
        rem_copy(ref, ref, x_send.at[i], x_recv.at[i], {"tm": me}).wait_recv()
    for s in range(N):
        k_rows[s * rows : (s + 1) * rows, :] = jnp.transpose(got[s, 0:HD, :])
        v_cols[:, s * rows : (s + 1) * rows] = got[s, HD : 2 * HD, :]
    cot.relay_far()

    factor = HD ** -0.5 * 1.4426950408889634
    pair = 2

    def attend(i):
        queries = jnp.concatenate(
            [got[i * pair + j, 2 * HD : 3 * HD, :] for j in range(pair)], axis=1
        )
        field = jnp.concatenate(
            [got[i * pair + j, 3 * HD : 4 * HD, :] for j in range(pair)], axis=1
        )
        scores = jnp.dot(k_rows[...], queries, preferred_element_type=F32)
        top = jnp.max(scores, axis=0, keepdims=True)
        expo = jnp.exp2(scores * factor - top * factor)
        total = jnp.sum(expo, axis=0, keepdims=True)
        summed = jnp.dot(v_cols[...], expo.astype(BF16), preferred_element_type=F32)
        attention = (summed / total).astype(BF16)
        block = field.astype(F32) + attention.astype(F32)
        cols = pl.ds(pl.multiple_of(i * pair * rows, pair * rows), pair * rows)
        mixed[:, cols] = block
        mean, square = own_stats(block)
        stats[me, 0:1, cols] = mean
        stats[me, 1:2, cols] = square

    half = N // pair // 2

    @pl.loop(0, half)
    def first(i):
        attend(i)

    cot.relay_near()

    @pl.loop(half, 2 * half)
    def second(i):
        attend(i)

    swap = Swap(me, stats, s_send, s_recv)
    swap.start()
    cot.relay_rest()
    swap.finish()
    mean, inv = joined_stats(stats)
    own_u[...] = ((mixed[...] - mean) * inv * gain_ref[...]).astype(BF16)
    ug = Gather(me, own_u, u_out, u_send, u_recv, keep_sem.at[2])
    ug.start()
    ug.relay_far()
    ug.relay_near()
    ug.relay_rest()
    cot.finish()
    for i in range(1, N):
        ref = w_out.at[lax.rem(me + N - i, N)]
        rem_copy(ref, ref, w_send.at[i], w_recv.at[i], {"tm": me}).wait_recv()
    for copy in x_copies + w_copies:
        copy.wait_send()
    w_keep.wait()
    ug.finish()


def vmem():
    return pl.BlockSpec(memory_space=pltpu.VMEM)


def anywhere():
    return pl.BlockSpec(memory_space=pl.ANY)


def front(query, keys, values, frames, w_parts, cot, gain):
    rows, width = query.shape
    length = rows * N
    dma = pltpu.SemaphoreType.DMA
    return pl.pallas_call(
        front_kernel,
        out_shape=(
            jax.ShapeDtypeStruct((N, HD, length), BF16),
            jax.ShapeDtypeStruct((N, rows, width), BF16),
            jax.ShapeDtypeStruct(w_parts.shape, BF16),
        ),
        in_specs=[vmem(), vmem(), vmem(), vmem(), anywhere(), anywhere(), vmem()],
        out_specs=(anywhere(), anywhere(), anywhere()),
        scratch_shapes=[
            pltpu.VMEM((N, 4 * HD, rows), BF16),
            pltpu.VMEM((N, 4 * HD, rows), BF16),
            pltpu.VMEM((length, HD), BF16),
            pltpu.VMEM((HD, length), BF16),
            pltpu.VMEM((HD, length), F32),
            pltpu.VMEM((N, 2, length), F32),
            pltpu.VMEM((HD, length), BF16),
            dma((N,)), dma((N,)), dma((N,)), dma((N,)), dma((N,)), dma((N,)),
            dma((15,)), dma((15,)), dma((15,)), dma((15,)), dma((3,)),
        ],
        compiler_params=pltpu.CompilerParams(
            collective_id=0, has_side_effects=True, vmem_limit_bytes=56 * 2**20
        ),
        name="front",
    )(query, keys, values, frames, w_parts, cot, gain)


def middle_kernel(
    p_ref, ds_ref, taps_ref, gain_ref,
    dp_out, s_out, taps_out,
    y_pad, z_cols, g_cols, dz_pad, stats, stats_e,
    s_send, s_recv, e_send, e_recv,
):
    me = lax.axis_index("tm")
    length = z_cols.shape[1]
    kernel = taps_ref.shape[0]
    half = kernel // 2
    step = 128
    blocks = length // step
    lanes = y_pad.shape[1]
    blank = jnp.zeros((lanes - HD, step), F32)

    edge = jnp.zeros((half, lanes), F32)
    for pad in (y_pad, dz_pad):
        pad[0:half, :] = edge
        pad[length + half : length + 2 * half, :] = edge

    @pl.loop(0, blocks)
    def gate(i):
        cols = pl.ds(pl.multiple_of(i * step, step), step)
        y = p_ref[0:HD, cols] * jax.nn.sigmoid(p_ref[HD : 2 * HD, cols])
        y = y.astype(BF16).astype(F32)
        y_pad[pl.ds(pl.multiple_of(half + i * step, half), step), :] = jnp.transpose(
            jnp.concatenate([y, blank], axis=0)
        )

    @pl.loop(0, blocks)
    def conv(i):
        start = pl.multiple_of(i * step, step)
        z = jnp.zeros((step, lanes), F32)
        for k in range(kernel):
            z = z + taps_ref[k : k + 1, :] * y_pad[pl.ds(start + k, step), :]
        z = jnp.transpose(z)[0:HD]
        cols = pl.ds(start, step)
        z_cols[:, cols] = z
        mean, square = own_stats(z)
        stats[me, 0:1, cols] = mean
        stats[me, 1:2, cols] = square

    tm_barrier(me)
    swap = Swap(me, stats, s_send, s_recv)
    swap.start()
    swap.finish()
    mean, inv = joined_stats(stats)
    gain = gain_ref[...]
    zhat = (z_cols[...] - mean) * inv
    z_cols[...] = zhat
    n = zhat * gain
    sgate = jax.nn.sigmoid(n)
    s_out[...] = (n * sgate).astype(BF16)
    e = ds_ref[...] * sgate * (1.0 + n * (1.0 - sgate)) * gain
    g_cols[...] = e
    stats_e[me, 0:1, :] = jnp.sum(e, axis=0, keepdims=True)
    stats_e[me, 1:2, :] = jnp.sum(e * zhat, axis=0, keepdims=True)
    swap_e = Swap(me, stats_e, e_send, e_recv)
    swap_e.start()
    swap_e.finish()
    sums = jnp.sum(stats_e[...], axis=0) * (1.0 / (N * HD))
    g_cols[...] = (
        ((g_cols[...] - sums[0:1] - z_cols[...] * sums[1:2]) * inv).astype(BF16).astype(F32)
    )

    @pl.loop(0, blocks)
    def turn(i):
        cols = pl.ds(pl.multiple_of(i * step, step), step)
        dz_pad[pl.ds(pl.multiple_of(half + i * step, half), step), :] = jnp.transpose(
            jnp.concatenate([g_cols[:, cols], blank], axis=0)
        )

    taps_out[...] = jnp.zeros_like(taps_out)

    @pl.loop(0, blocks)
    def back(i):
        start = pl.multiple_of(i * step, step)
        dy = jnp.zeros((step, lanes), F32)
        for k in range(kernel):
            dy = dy + taps_ref[k : k + 1, :] * dz_pad[pl.ds(start + 2 * half - k, step), :]
        dy = jnp.transpose(dy)[0:HD]
        cols = pl.ds(start, step)
        pa = p_ref[0:HD, cols]
        sig = jax.nn.sigmoid(p_ref[HD : 2 * HD, cols])
        dp_out[0:HD, cols] = (dy * sig).astype(BF16)
        dp_out[HD : 2 * HD, cols] = (dy * pa * sig * (1.0 - sig)).astype(BF16)
        dz = dz_pad[pl.ds(pl.multiple_of(half + start, half), step), :]
        for k in range(kernel):
            prod = dz * y_pad[pl.ds(start + k, step), :]
            taps_out[k : k + 1, :] += jnp.sum(prod, axis=0, keepdims=True)


def middle(p_cols, ds_cols, taps, gain):
    length = p_cols.shape[1]
    kernel, lanes = taps.shape
    dma = pltpu.SemaphoreType.DMA
    return pl.pallas_call(
        middle_kernel,
        out_shape=(
            jax.ShapeDtypeStruct((2 * HD, length), BF16),
            jax.ShapeDtypeStruct((HD, length), BF16),
            jax.ShapeDtypeStruct((kernel, lanes), F32),
        ),
        in_specs=[vmem()] * 4,
        out_specs=(vmem(), vmem(), vmem()),
        scratch_shapes=[
            pltpu.VMEM((length + kernel, lanes), F32),
            pltpu.VMEM((HD, length), F32),
            pltpu.VMEM((HD, length), F32),
            pltpu.VMEM((length + kernel, lanes), F32),
            pltpu.VMEM((N, 2, length), F32),
            pltpu.VMEM((N, 2, length), F32),
            dma((N,)), dma((N,)), dma((N,)), dma((N,)),
        ],
        compiler_params=pltpu.CompilerParams(
            collective_id=1, has_side_effects=True, vmem_limit_bytes=56 * 2**20
        ),
        name="middle",
    )(p_cols, ds_cols, taps, gain)


def reduce_kernel(
    g_ref, o_ref, t_ref, g_out, o_out, t_out,
    g_got, o_got, t_got, g_red, o_red,
    gs, gr, os, orr, ts, tr, g2s, g2r, o2s, o2r,
):
    d = lax.axis_index("dp")
    t = lax.axis_index("tm")
    barrier = pltpu.get_barrier_semaphore()

    def greet(dp, tm):
        pl.semaphore_signal(
            barrier, inc=1, device_id={"dp": dp, "tm": tm}, device_id_type=MESH
        )

    for i in range(1, N):
        peer = lax.rem(d + i, N)
        greet(peer, t)
        greet(peer, d)
        greet(t, lax.rem(t + i, N))

    @pl.when(t != d)
    def _():
        greet(d, d)
        greet(t, t)

    pl.semaphore_wait(barrier, jnp.where(t == d, 3 * (N - 1), 3 * (N - 1) + 2))

    first = []
    for i in range(1, N):
        peer = lax.rem(d + i, N)
        to = {"dp": peer, "tm": t}
        first.append(rem_copy(g_ref.at[peer], g_got.at[d], gs.at[i], gr.at[i], to))
        first.append(rem_copy(o_ref.at[peer], o_got.at[d], os.at[i], orr.at[i], to))
        first.append(rem_copy(t_ref, t_got.at[d], ts.at[i], tr.at[i], to))
        for copy in first[-3:]:
            copy.start()
    g_got[d] = g_ref[d]
    o_got[d] = o_ref[d]
    t_got[d] = t_ref[...]
    here = {"dp": d, "tm": t}
    for i in range(1, N):
        slot = lax.rem(d + N - i, N)
        for buf, send, recv in ((g_got, gs, gr), (o_got, os, orr), (t_got, ts, tr)):
            rem_copy(buf.at[slot], buf.at[slot], send.at[i], recv.at[i], here).wait_recv()
    g_red[...] = jnp.sum(g_got[...].astype(F32), axis=0).astype(BF16)
    o_red[...] = jnp.sum(o_got[...].astype(F32), axis=0).astype(BF16)
    t_out[...] = jnp.sum(t_got[...].astype(F32), axis=0)

    second = []
    for i in range(1, N):
        peer = lax.rem(d + i, N)
        second.append(
            rem_copy(g_red, g_out.at[t], g2s.at[i], g2r.at[t], {"dp": peer, "tm": d})
        )
        second.append(
            rem_copy(o_red, o_out.at[d], o2s.at[i], o2r.at[i], {"dp": peer, "tm": t})
        )
        second[-2].start()
        second[-1].start()
    last = rem_copy(g_red, g_out.at[t], g2s.at[0], g2r.at[t], {"dp": d, "tm": d})

    @pl.when(t != d)
    def _():
        last.start()

    @pl.when(t == d)
    def _():
        g_out[t] = g_red[...]

    o_out[d] = o_red[...]
    for i in range(1, N):
        slot = lax.rem(d + N - i, N)
        ref = o_out.at[slot]
        rem_copy(ref, ref, o2s.at[i], o2r.at[i], here).wait_recv()
        slot = lax.rem(t + i, N)
        ref = g_out.at[slot]
        rem_copy(ref, ref, g2s.at[i], g2r.at[slot], here).wait_recv()

    @pl.when(t != d)
    def _():
        ref = g_out.at[t]
        rem_copy(ref, ref, g2s.at[0], g2r.at[t], here).wait_recv()
        last.wait_send()

    for copy in first + second:
        copy.wait_send()


def reduce_all(g_parts, o_parts, t_part):
    dma = pltpu.SemaphoreType.DMA
    return pl.pallas_call(
        reduce_kernel,
        out_shape=(
            jax.ShapeDtypeStruct(g_parts.shape, BF16),
            jax.ShapeDtypeStruct(o_parts.shape, BF16),
            jax.ShapeDtypeStruct(t_part.shape, F32),
        ),
        in_specs=[vmem()] * 3,
        out_specs=(vmem(), vmem(), vmem()),
        scratch_shapes=[
            pltpu.VMEM(g_parts.shape, BF16),
            pltpu.VMEM(o_parts.shape, BF16),
            pltpu.VMEM((N,) + t_part.shape, BF16),
            pltpu.VMEM(g_parts.shape[1:], BF16),
            pltpu.VMEM(o_parts.shape[1:], BF16),
        ] + [dma((N,))] * 10,
        compiler_params=pltpu.CompilerParams(
            collective_id=2, has_side_effects=True, vmem_limit_bytes=56 * 2**20
        ),
        name="reduce_all",
    )(g_parts, o_parts, t_part)


def local(frames, query, keys, values, norm_gain, conv_gain, w_glu, taps, w_out, cotangent):
    rows, width = frames.shape[1:]
    length = rows * N
    t = lax.axis_index("tm")
    own = lambda gain: lax.dynamic_slice_in_dim(gain, t * HD, HD).reshape(HD, 1)
    w_parts = w_glu.reshape(HD, 2, N, HD).transpose(2, 0, 1, 3).reshape(N, HD, 2 * HD)
    u_all, cot_all, w_cols = front(
        query[0], keys[0], values[0], frames[0], w_parts, cotangent[0], own(norm_gain)
    )
    u_cols = u_all.reshape(width, length)
    cot_rows = cot_all.reshape(length, width)
    p_cols = lax.dot_general(
        w_cols.reshape(width, 2 * HD), u_cols, (((0,), (0,)), ((), ())), preferred_element_type=F32
    )
    ds_cols = lax.dot_general(
        w_out, cot_rows, (((1,), (1,)), ((), ())), preferred_element_type=F32
    )
    own_taps = jnp.pad(lax.dynamic_slice_in_dim(taps, t * HD, HD, axis=1), ((0, 0), (0, 128 - HD)))
    dp_cols, s_cols, taps_part = middle(p_cols, ds_cols, own_taps, own(conv_gain))
    g_part = lax.dot_general(
        u_cols, dp_cols, (((1,), (1,)), ((), ())), preferred_element_type=F32
    ).astype(BF16)
    o_part = lax.dot_general(
        s_cols, cot_rows, (((1,), (0,)), ((), ())), preferred_element_type=F32
    ).astype(BF16)
    g_all, o_all, t_all = reduce_all(
        g_part.reshape(N, HD, 2 * HD),
        o_part.reshape(HD, N, HD).transpose(1, 0, 2),
        taps_part.astype(BF16),
    )
    glu_grad = g_all.reshape(N, HD, 2, HD).transpose(1, 2, 0, 3).reshape(HD, 2 * width).astype(F32)
    out_grad = o_all.transpose(1, 0, 2).reshape(HD, width).astype(F32)
    return glu_grad, t_all[:, :HD], out_grad


def solution(mesh):
    return jax.shard_map(
        local,
        mesh=mesh,
        in_specs=(
            P("dp", "tm", None),
            P("dp", "tm", None),
            P("dp", "tm", None),
            P("dp", "tm", None),
            P(),
            P(),
            P("tm", None),
            P(),
            P("tm", None),
            P("dp", "tm", None),
        ),
        out_specs=(P("tm", None), P(None, "tm"), P("tm", None)),
        check_vma=False,
    )
```

time: 735 us -> 286 us (0.39)
  waiting for transfers between devices: 548 us -> 0 us
  Pallas kernels: 0 us -> 245 us
  starting transfers between devices: 47.3 us -> 0 us
  other arithmetic: 37.7 us -> 1.67 us
  blocking collectives: 35.8 us -> 0 us
  between operations: 15.3 us -> 0.83 us
  matrix products: 25.4 us -> 15.6 us
    pallas_call x0 -> x3, Pallas kernels: none -> 245 us  [the longest x1 129 us: front(): pl.pallas_call(front_kernel, out_shape=(jax.ShapeDtypeStruct((N, HD, leng...]
    reduce_scatter x2 -> x0, waiting for transfers between devices: 224 us -> none  [the longest x1 153 us: local(): lax.psum_scatter(glu_term.astype(jnp.bfloat16), 'tm', scatter_dimension=0...]
    psum x1 -> x0, waiting for transfers between devices: 118 us -> none  [local(): lax.psum(glu_share.astype(jnp.bfloat16), 'dp').astype(jnp.float32)]
    unnamed x7 -> x0, waiting for transfers between devices: 77.6 us -> none
    all_to_all x4 -> x0, waiting for transfers between devices: 62.7 us -> none  [the longest x1 26.2 us: local(): lax.all_to_all(heads_out, 'tm', split_axis=0, concat_axis=1, tiled=True)]
    all_gather x2 -> x0, waiting for transfers between devices: 57.5 us -> none  [the longest x1 55.5 us: local(): lax.all_gather(w_out, 'tm', axis=0, tiled=True)]
    psum x1 -> x0, blocking collectives: 35.8 us -> none  [local(): lax.psum(taps_share.astype(jnp.bfloat16), 'dp').astype(jnp.float32)]
    all_to_all x4 -> x0, starting transfers between devices: 30.6 us -> none  [the longest x1 12.6 us: local(): lax.all_to_all(split_heads(query), 'tm', split_axis=1, concat_axis=0, til...]
  transfers between devices with their start and end apart: 14 -> 0, of which waited for: 12 -> 0; matrix products, arithmetic and copies ran while one was open for 10% -> 0% of each run, Pallas kernels for 0% -> 0%
where the time goes in v1:
time: 286 us; the launch traced here: 281 us
  Pallas kernels  245 us (86%)
  local copies, waits for them, and re-layouts  17.5 us (6%)
  matrix products  15.6 us (5%)
    pallas_call x1, Pallas kernels, front(): pl.pallas_call(front_kernel, out_shape=(jax.ShapeDtypeStruct((N, HD, leng...  129 us
    pallas_call x1, Pallas kernels, reduce_all(): pl.pallas_call(reduce_kernel, out_shape=(jax.ShapeDtypeStruct(g_parts.sha...  82.3 us
    pallas_call x1, Pallas kernels, middle(): pl.pallas_call(middle_kernel, out_shape=(jax.ShapeDtypeStruct((2 * HD, le...  33.8 us
    dot_general x1, matrix products, local(): lax.dot_general(w_out, cot_rows, (((1,), (1,)), ((), ())), preferred_elem...  5.83 us

profile of v1, /device:TPU:1, one launch (start us, length us, event | category | flops | bytes accessed | tf_op | source)
XLA Modules:
  0.0 281.1 jit_solution(16966979560107227900)
XLA Ops:
  0.6 0.0 copy-start
  0.7 0.8 dynamic-slice_bitcast_fusion
  1.5 0.8 constant_dynamic-slice_fusion
  2.3 0.6 pad.4.taps_ref
  2.9 0.7 copy.22.gain_ref
  3.7 0.7 copy.20.gain_ref
  4.4 1.9 reshape.40
  6.3 0.8 copy.30
  7.0 1.3 reshape.41.w_ref
  8.4 129.4 %front.1 = (bf16[16,96,2048]{2,1,0:T(8,128)(2,1)}, bf16[16,128,1536]{2,1,0:T(8,128)(2,1)}, bf16[16,96,192]{2,1,0:T(8,128)(2,1)}) custom-call(bf16[128,1536]{1,0:T(8,128)(2,1)} %bitcast.45, bf16[128,1536]{1,0:T(8,128)(2,1)} %bitcast.46, bf16[128,1536]{1,0:T(8,128)(2,1)} %bitcast.47, bf16[128,1536]{1,0:T(8,128)(2,1)} %bitcast.48, ...), custom_call_target="tpu_custom_call" | custom-call | tf_op jit(solution)/shard_map/front/pallas_call | solution.py:243
  137.7 0.0 copy-start.1
  137.7 0.0 copy-start.2
  137.8 0.0 copy-done
  137.8 0.0 slice-start
  137.8 5.8 %convolution_bitcast_fusion.1.ds_ref = f32[96,2048]{1,0:T(8,128)} fusion(bf16[2048,1536]{1,0:T(8,128)(2,1)} %bitcast.36, bf16[96,1536]{1,0:T(8,128)(2,1)S(1)} %copy-done), kind=kOutput, calls=%fused_computation.2 | convolution fusion | flops 603979776 | bytes 7372800 | tf_op jit(solution)/shard_map/dot_general | solution.py:518
  143.6 0.0 copy-done.1
  143.6 0.0 copy-done.2
  143.6 0.0 slice-start.1
  143.6 2.6 convolution_bitcast_fusion.p_ref
  146.2 33.8 %middle.1 = (bf16[192,2048]{1,0:T(8,128)(2,1)}, bf16[96,2048]{1,0:T(8,128)(2,1)}, f32[32,128]{1,0:T(8,128)}) custom-call(f32[192,2048]{1,0:T(8,128)} %convolution_bitcast_fusion.p_ref, f32[96,2048]{1,0:T(8,128)} %convolution_bitcast_fusion.1.ds_ref, f32[32,128]{1,0:T(8,128)} %pad.4.taps_ref, f32[96,1]{1,0:T(8,128)} %copy.22.gain_ref), custom_call_target="tpu_custom_call" | custom-call | tf_op jit(solution)/shard_map/middle/pallas_call | solution.py:366
  180.0 0.0 copy-start.5
  180.1 0.0 slice-done
  180.1 0.0 slice-done.1
  180.1 2.2 convolution_convert_fusion.1
  182.3 0.0 copy-start.3
  182.3 0.0 copy-done.5
  182.3 5.0 %convolution_convert_fusion = bf16[1536,192]{0,1:T(8,128)(2,1)S(1)} fusion(bf16[1536,2048]{1,0:T(8,128)(2,1)} %bitcast.40, bf16[192,2048]{1,0:T(8,128)(2,1)S(1)} %copy-done.5), kind=kOutput, calls=%fused_computation.1 | convolution fusion | flops 1208254464 | bytes 7667712 | tf_op jit(solution)/shard_map/dot_general | solution.py:523
  187.3 0.0 copy-done.3
  187.3 0.6 convert_element_type.34.t_ref
  187.9 0.3 reshape.47
  188.2 0.8 copy.31
  189.1 1.2 copy.23
  190.2 82.3 %reduce_all.1 = (bf16[16,96,192]{2,1,0:T(8,128)(2,1)}, bf16[16,96,96]{2,1,0:T(8,128)(2,1)}, f32[32,128]{1,0:T(8,128)}) custom-call(bf16[16,96,192]{2,1,0:T(8,128)(2,1)} %bitcast.43, bf16[16,96,96]{2,1,0:T(8,128)(2,1)} %bitcast.44, bf16[32,128]{1,0:T(8,128)(2,1)} %convert_element_type.34.t_ref), custom_call_target="tpu_custom_call" | custom-call | tf_op jit(solution)/shard_map/reduce_all/pallas_call | solution.py:481
  272.5 0.0 copy-start.4
  272.5 2.4 reshape.50
  275.0 0.9 copy.25
  275.9 1.9 reshape.48
  277.8 1.1 convert_bitcast_fusion
  278.9 0.5 copy.26
  279.4 1.1 reshape.49
  280.5 0.0 copy-done.4
  280.5 0.6 copy.33
  (1 shorter events, 0.0 us)
Async XLA Ops:
  0.6 137.1 %copy-start = (bf16[96,1536]{1,0:T(8,128)(2,1)S(1)}, bf16[96,1536]{1,0:T(8,128)(2,1)}, u32[]{:S(2)}) copy-start(bf16[96,1536]{1,0:T(8,128)(2,1)} %param.18) | copy-start | bytes 884740
  137.7 5.9 %copy-start.1 = (bf16[16,96,2048]{2,1,0:T(8,128)(2,1)S(1)}, bf16[16,96,2048]{2,1,0:T(8,128)(2,1)}, u32[]{:S(2)}) copy-start(bf16[16,96,2048]{2,1,0:T(8,128)(2,1)} %get-tuple-element.12) | copy-start | bytes 18874372
  137.7 5.9 %copy-start.2 = (bf16[16,96,192]{2,1,0:T(8,128)(2,1)S(1)}, bf16[16,96,192]{2,1,0:T(8,128)(2,1)}, u32[]{:S(2)}) copy-start(bf16[16,96,192]{2,1,0:T(8,128)(2,1)} %get-tuple-element.13) | copy-start | bytes 1769476
  137.8 42.3 %slice-start = ((s8[6291456]{0:T(1024)(128)(4,1)}), s8[4194304]{0:T(1024)(128)(4,1)S(1)}, s32[]{:S(2)}) async-start(s8[6291456]{0:T(1024)(128)(4,1)} %bitcast.37), calls=%async_computation | async-start | bytes 8388608
  143.6 36.5 %slice-start.1 = ((s8[6291456]{0:T(1024)(128)(4,1)}), s8[2097152]{0:T(1024)(128)(4,1)S(1)}, s32[]{:S(2)}) async-start(s8[6291456]{0:T(1024)(128)(4,1)} %bitcast.37), calls=%async_computation.1 | async-start | bytes 4194304
  180.0 2.2 copy-start.5
  182.3 5.0 %copy-start.3 = (f32[32,128]{1,0:T(8,128)S(1)}, f32[32,128]{1,0:T(8,128)}, u32[]{:S(2)}) copy-start(f32[32,128]{1,0:T(8,128)} %get-tuple-element.17) | copy-start | bytes 49156
  272.5 8.0 %copy-start.4 = (f32[32,128]{1,0:T(8,128)S(1)}, f32[32,128]{1,0:T(8,128)}, u32[]{:S(2)}) copy-start(f32[32,128]{1,0:T(8,128)} %get-tuple-element.19) | copy-start | bytes 49156

commit v2 on v1

v2 whole, which is shorter than its diff:
```python
import functools

import jax
import jax.numpy as jnp
from jax import lax
from jax.experimental import pallas as pl
from jax.experimental.pallas import tpu as pltpu
from jax.sharding import PartitionSpec as P

N = 16
HD = 96
MESH = pl.DeviceIdType.MESH
F32 = jnp.float32
BF16 = jnp.bfloat16
EPS = 1e-05


def rem_copy(src, dst, send, recv, peer):
    return pltpu.make_async_remote_copy(
        src_ref=src, dst_ref=dst, send_sem=send, recv_sem=recv, device_id=peer, device_id_type=MESH
    )


class Gather:
    def __init__(self, me, own, out, slot, send, recv):
        self.own, self.out, self.slot, self.send, self.recv = own, out, slot, send, recv
        y = me // 4
        z = lax.rem(me // 2, 2)
        c = lax.rem(me, 2)
        at = lambda yy, zz, cc: lax.rem(yy, 4) * 4 + zz * 2 + cc
        self.me = me
        self.far = at(y, 1 - z, c)
        self.sib = at(y, z, 1 - c)
        self.to = [at(y + j, z, c) for j in range(1, 4)]
        self.frm = [at(y + 4 - j, z, c) for j in range(1, 4)]
        self.frm_far = [at(y + 4 - j, 1 - z, c) for j in range(1, 4)]
        self.frm_sib = (
            [self.sib, at(y, 1 - z, 1 - c)]
            + [at(y + 4 - j, z, 1 - c) for j in range(1, 4)]
            + [at(y + 4 - j, 1 - z, 1 - c) for j in range(1, 4)]
        )
        self.started = []

    def go(self, src, block, sem, peer):
        copy = rem_copy(
            src, self.out.at[self.slot(block)], self.send.at[sem], self.recv.at[sem], {"tm": peer}
        )
        copy.start()
        self.started.append(copy)

    def on(self, block, sem, peer):
        self.go(self.out.at[self.slot(block)], block, sem, peer)

    def landed(self, block, sem):
        ref = self.out.at[self.slot(block)]
        rem_copy(ref, ref, self.send.at[sem], self.recv.at[sem], {"tm": self.sib}).wait_recv()

    def start(self):
        self.go(self.own, self.me, 0, self.far)
        for j in (0, 2, 1):
            self.go(self.own, self.me, 1 + j, self.to[j])
        self.go(self.own, self.me, 7, self.sib)

    def relay_far(self):
        self.landed(self.far, 0)
        for j in (0, 2, 1):
            self.on(self.far, 4 + j, self.to[j])
        self.on(self.far, 8, self.sib)

    def relay_near(self):
        for j in (0, 2, 1):
            self.landed(self.frm[j], 1 + j)
            self.on(self.frm[j], 9 + j, self.sib)

    def relay_rest(self):
        for j in (0, 2, 1):
            self.landed(self.frm_far[j], 4 + j)
            self.on(self.frm_far[j], 12 + j, self.sib)

    def near_from_sibling(self):
        for k in (0, 2, 3, 4):
            self.landed(self.frm_sib[k], 7 + k)

    def rest_from_sibling(self):
        for k in (1, 5, 6, 7):
            self.landed(self.frm_sib[k], 7 + k)

    def sent(self):
        for copy in self.started:
            copy.wait_send()


class Swap:
    def __init__(self, me, buf, send, recv):
        self.me, self.buf, self.send, self.recv = me, buf, send, recv
        self.started = []

    def start(self):
        for i in range(1, N):
            copy = rem_copy(
                self.buf.at[self.me],
                self.buf.at[self.me],
                self.send.at[i],
                self.recv.at[i],
                {"tm": lax.rem(self.me + i, N)},
            )
            copy.start()
            self.started.append(copy)

    def finish(self):
        for i in range(1, N):
            ref = self.buf.at[lax.rem(self.me + N - i, N)]
            rem_copy(ref, ref, self.send.at[i], self.recv.at[i], {"tm": self.me}).wait_recv()
        for copy in self.started:
            copy.wait_send()


def own_stats(x):
    mean = jnp.mean(x, axis=0, keepdims=True)
    dev = x - mean
    return mean, jnp.sum(dev * dev, axis=0, keepdims=True)


def joined_stats(buf):
    means = buf[:, 0, :]
    squares = buf[:, 1, :]
    mean = jnp.mean(means, axis=0, keepdims=True)
    dev = means - mean
    total = jnp.sum(squares, axis=0, keepdims=True) + HD * jnp.sum(dev * dev, axis=0, keepdims=True)
    return mean, lax.rsqrt(total * (1.0 / (N * HD)) + EPS)


def core_kernel(
    q_ref, k_ref, v_ref, f_ref, wg_ref, wo_ref, cot_ref, taps_ref, ng_ref, cg_ref,
    glu_out, out_out, taps_out,
    kv_own, qf_own, kv, qf, k_rows, v_cols, mixed, stats, stats_z, stats_e,
    w_own, w_got, u_all, cot_all, small, taps_own, p, ds, y_pad, dz_pad, z_cols, g_cols, s_cols, dp,
    t_own, g_own, o_own, g_got, o_got, t_got, g_red, o_red, g_fin, o_fin,
    kv_s, kv_r, qf_s, qf_r, w_s, w_r, st_s, st_r, sz_s, sz_r, se_s, se_r,
    c_s, c_r, u_s, u_r, g1_s, g1_r, o1_s, o1_r, t1_s, t1_r, g2_s, g2_r, o2_s, o2_r, own_sem,
):
    d = lax.axis_index("dp")
    t = lax.axis_index("tm")
    rows = q_ref.shape[0]
    length = mixed.shape[1]
    kernel = taps_ref.shape[0]
    half = kernel // 2
    y_at = t // 4
    group = lax.rem(t, 4)
    place = lambda block: lax.rem(block, 4) * 4 + block // 4

    barrier = pltpu.get_barrier_semaphore()

    def greet(dp_at, tm_at):
        pl.semaphore_signal(
            barrier, inc=1, device_id={"dp": dp_at, "tm": tm_at}, device_id_type=MESH
        )

    for i in range(1, N):
        greet(d, lax.rem(t + i, N))
        greet(lax.rem(d + i, N), t)
        greet(lax.rem(d + i, N), d)
        greet(t, lax.rem(t + i, N))

    @pl.when(t != d)
    def _():
        greet(d, d)
        greet(t, t)

    def turn_into(ref, buf, a):
        turned = jnp.transpose(ref[...])
        for j in range(N):
            buf[j, a * HD : (a + 1) * HD, :] = turned[j * HD : (j + 1) * HD]

    sent = []

    def scatter(src, dst, slot, send, recv):
        for i in range(1, N):
            peer = lax.rem(t + i, N)
            copy = rem_copy(src.at[peer], dst.at[slot], send.at[i], recv.at[i], {"tm": peer})
            copy.start()
            sent.append(copy)

    def arrived(dst, slot, i, send, recv):
        ref = dst.at[slot]
        rem_copy(ref, ref, send.at[i], recv.at[i], {"tm": t}).wait_recv()

    turn_into(k_ref, kv_own, 0)
    turn_into(v_ref, kv_own, 1)
    cot_keep = pltpu.make_async_copy(cot_ref, cot_all.at[t], own_sem)
    cot_keep.start()
    pl.semaphore_wait(barrier, jnp.where(t == d, 4 * (N - 1), 4 * (N - 1) + 2))
    scatter(kv_own, kv, t, kv_s, kv_r)
    turn_into(q_ref, qf_own, 0)
    turn_into(f_ref, qf_own, 1)
    scatter(qf_own, qf, t, qf_s, qf_r)
    width = N * HD
    for j in range(N):
        w_own[j] = jnp.concatenate(
            [
                wg_ref[:, j * HD : (j + 1) * HD],
                wg_ref[:, width + j * HD : width + (j + 1) * HD],
            ],
            axis=1,
        )
    scatter(w_own, w_got, place(t), w_s, w_r)
    kv[t] = kv_own[t]
    qf[t] = qf_own[t]
    w_got[place(t)] = w_own[t]

    small[...] = jnp.transpose(
        jnp.concatenate(
            [
                taps_ref[...],
                ng_ref[...],
                cg_ref[...],
                jnp.zeros((128 - kernel - 2, width), F32),
            ],
            axis=0,
        )
    )
    mine = small[pl.ds(pl.multiple_of(t * HD, HD), HD), :]
    lanes = taps_own.shape[1]
    blank = jnp.zeros((lanes - HD, 128), F32)
    taps_own[...] = jnp.transpose(jnp.concatenate([mine, blank], axis=0))[0:kernel]
    norm_gain = mine[:, kernel : kernel + 1]
    conv_gain = mine[:, kernel + 1 : kernel + 2]
    edge = jnp.zeros((half, lanes), F32)
    for pad in (y_pad, dz_pad):
        pad[0:half, :] = edge
        pad[length + half : length + 2 * half, :] = edge

    for i in range(1, N):
        arrived(kv, lax.rem(t + N - i, N), i, kv_s, kv_r)
    for s in range(N):
        k_rows[s * rows : (s + 1) * rows, :] = jnp.transpose(kv[s, 0:HD, :])
        v_cols[:, s * rows : (s + 1) * rows] = kv[s, HD : 2 * HD, :]
    cot = Gather(t, cot_ref, cot_all, lambda block: block, c_s, c_r)
    cot.start()

    factor = HD ** -0.5 * 1.4426950408889634
    pair = 2

    @pl.loop(0, N // pair)
    def attend(i):
        for j in range(pair):
            s = i * pair + j

            @pl.when(s != t)
            def _():
                arrived(qf, s, lax.rem(t + N - s, N), qf_s, qf_r)

        queries = jnp.concatenate([qf[i * pair + j, 0:HD, :] for j in range(pair)], axis=1)
        field = jnp.concatenate([qf[i * pair + j, HD : 2 * HD, :] for j in range(pair)], axis=1)
        scores = jnp.dot(k_rows[...], queries, preferred_element_type=F32)
        top = jnp.max(scores, axis=0, keepdims=True)
        expo = jnp.exp2(scores * factor - top * factor)
        total = jnp.sum(expo, axis=0, keepdims=True)
        summed = jnp.dot(v_cols[...], expo.astype(BF16), preferred_element_type=F32)
        attention = (summed / total).astype(BF16)
        block = field.astype(F32) + attention.astype(F32)
        cols = pl.ds(pl.multiple_of(i * pair * rows, pair * rows), pair * rows)
        mixed[:, cols] = block
        mean, square = own_stats(block)
        stats[t, 0:1, cols] = mean
        stats[t, 1:2, cols] = square

    swap = Swap(t, stats, st_s, st_r)
    swap.start()
    cot.relay_near()
    swap.finish()
    mean, inv = joined_stats(stats)
    u_all[place(t)] = ((mixed[...] - mean) * inv * norm_gain).astype(BF16)
    ug = Gather(t, u_all.at[place(t)], u_all, place, u_s, u_r)
    ug.start()

    def back_rows(z):
        @pl.loop(0, 4)
        def _(yy):
            first = yy * 4 + z * 2
            block = cot_all[pl.ds(first, 2)].reshape(2 * rows, width)
            ds[:, pl.ds(pl.multiple_of(first * rows, 2 * rows), 2 * rows)] = lax.dot_general(
                wo_ref[...], block, (((1,), (1,)), ((), ())), preferred_element_type=F32
            )

    z_at = lax.rem(t // 2, 2)
    cot.near_from_sibling()
    cot_keep.wait()
    back_rows(z_at)

    for i in range(1, N):
        arrived(w_got, place(lax.rem(t + N - i, N)), i, w_s, w_r)
    chunk = 512

    def product(g, first):
        weights = w_got[pl.ds(g * 4, 4)].reshape(4 * HD, 2 * HD)

        @pl.loop(0, length // chunk)
        def _(i):
            cols = pl.ds(pl.multiple_of(i * chunk, chunk), chunk)
            part = u_all[pl.ds(g * 4, 4), :, cols].reshape(4 * HD, chunk)
            part = lax.dot_general(
                weights, part, (((0,), (0,)), ((), ())), preferred_element_type=F32
            )
            p[:, cols] = part if first else p[:, cols] + part

    side = lax.rem(group + 1, 2) - lax.rem(group, 2)
    ug.relay_far()
    ug.relay_near()
    product(group, True)
    ug.near_from_sibling()
    product(group + side, False)
    ug.relay_rest()
    cot.relay_far()
    other = lax.rem(group + 2, 4)
    product(other, False)
    ug.rest_from_sibling()
    product(other + side, False)

    step = 128
    blocks = length // step

    @pl.loop(0, blocks)
    def gate(i):
        cols = pl.ds(pl.multiple_of(i * step, step), step)
        y = p[0:HD, cols] * jax.nn.sigmoid(p[HD : 2 * HD, cols])
        y = y.astype(BF16).astype(F32)
        y_pad[pl.ds(pl.multiple_of(half + i * step, half), step), :] = jnp.transpose(
            jnp.concatenate([y, blank], axis=0)
        )

    @pl.loop(0, blocks)
    def conv(i):
        start = pl.multiple_of(i * step, step)
        z = jnp.zeros((step, lanes), F32)
        for k in range(kernel):
            z = z + taps_own[k : k + 1, :] * y_pad[pl.ds(start + k, step), :]
        z = jnp.transpose(z)[0:HD]
        cols = pl.ds(start, step)
        z_cols[:, cols] = z
        mean, square = own_stats(z)
        stats_z[t, 0:1, cols] = mean
        stats_z[t, 1:2, cols] = square

    swap = Swap(t, stats_z, sz_s, sz_r)
    swap.start()
    cot.relay_rest()
    cot.rest_from_sibling()
    back_rows(1 - z_at)
    swap.finish()
    mean, inv = joined_stats(stats_z)
    zhat = (z_cols[...] - mean) * inv
    z_cols[...] = zhat
    n = zhat * conv_gain
    sgate = jax.nn.sigmoid(n)
    s_cols[...] = (n * sgate).astype(BF16)
    e = ds[...] * sgate * (1.0 + n * (1.0 - sgate)) * conv_gain
    g_cols[...] = e
    stats_e[t, 0:1, :] = jnp.sum(e, axis=0, keepdims=True)
    stats_e[t, 1:2, :] = jnp.sum(e * zhat, axis=0, keepdims=True)
    swap_e = Swap(t, stats_e, se_s, se_r)
    swap_e.start()

    for j in range(4):
        cols = slice(j * 4 * HD, (j + 1) * 4 * HD)
        part = jnp.dot(
            s_cols[...], cot_all[:, :, cols].reshape(length, 4 * HD), preferred_element_type=F32
        ).astype(BF16)
        for k in range(4):
            o_own[4 * j + k] = part[:, k * HD : (k + 1) * HD]
    for i in range(1, N):
        peer = lax.rem(d + i, N)
        copy = rem_copy(o_own.at[peer], o_got.at[d], o1_s.at[i], o1_r.at[i], {"dp": peer, "tm": t})
        copy.start()
        sent.append(copy)
    o_got[d] = o_own[d]

    swap_e.finish()
    sums = jnp.sum(stats_e[...], axis=0) * (1.0 / (N * HD))
    g_cols[...] = (
        ((g_cols[...] - sums[0:1] - z_cols[...] * sums[1:2]) * inv).astype(BF16).astype(F32)
    )

    @pl.loop(0, blocks)
    def turn(i):
        cols = pl.ds(pl.multiple_of(i * step, step), step)
        dz_pad[pl.ds(pl.multiple_of(half + i * step, half), step), :] = jnp.transpose(
            jnp.concatenate([g_cols[:, cols], blank], axis=0)
        )

    t_own[...] = jnp.zeros_like(t_own)

    @pl.loop(0, blocks)
    def back(i):
        start = pl.multiple_of(i * step, step)
        dy = jnp.zeros((step, lanes), F32)
        for k in range(kernel):
            dy = dy + taps_own[k : k + 1, :] * dz_pad[pl.ds(start + 2 * half - k, step), :]
        dy = jnp.transpose(dy)[0:HD]
        cols = pl.ds(start, step)
        pa = p[0:HD, cols]
        sig = jax.nn.sigmoid(p[HD : 2 * HD, cols])
        dp[0:HD, cols] = (dy * sig).astype(BF16)
        dp[HD : 2 * HD, cols] = (dy * pa * sig * (1.0 - sig)).astype(BF16)
        dz = dz_pad[pl.ds(pl.multiple_of(half + start, half), step), :]
        for k in range(kernel):
            prod = dz * y_pad[pl.ds(start + k, step), :]
            t_own[k : k + 1, :] += jnp.sum(prod, axis=0, keepdims=True)

    @pl.loop(0, 4)
    def grads(i):
        g = lax.rem(i + d, 4)
        part = lax.dot_general(
            u_all[pl.ds(g * 4, 4)].reshape(4 * HD, length),
            dp[...],
            (((1,), (1,)), ((), ())),
            preferred_element_type=F32,
        ).astype(BF16)
        for j in range(4):
            block = part[j * HD : (j + 1) * HD]
            owner = 4 * j + g
            g_own[owner, 0:HD, :] = block[:, 0:128]
            g_own[owner, HD : HD + HD // 2, :] = jnp.concatenate(
                [block[0 : HD // 2, 128:], block[HD // 2 :, 128:]], axis=1
            )

            @pl.when(owner != d)
            def _():
                rem_copy(
                    g_own.at[owner], g_got.at[d], g1_s.at[owner], g1_r.at[d], {"dp": owner, "tm": t}
                ).start()

    g_got[d] = g_own[d]
    t_got[d] = t_own[...].astype(BF16)
    for i in range(1, N):
        peer = lax.rem(d + i, N)
        copy = rem_copy(t_got.at[d], t_got.at[d], t1_s.at[i], t1_r.at[i], {"dp": peer, "tm": t})
        copy.start()
        sent.append(copy)

    here = {"dp": d, "tm": t}

    def dp_arrived(buf, slot, send, recv, i):
        ref = buf.at[slot]
        rem_copy(ref, ref, send.at[i], recv.at[i], here).wait_recv()

    for i in range(1, N):
        dp_arrived(o_got, lax.rem(d + N - i, N), o1_s, o1_r, i)
    o_red[...] = jnp.sum(o_got[...].astype(F32), axis=0).astype(BF16)
    for i in range(1, N):
        peer = lax.rem(d + i, N)
        copy = rem_copy(o_red, o_fin.at[d], o2_s.at[i], o2_r.at[i], {"dp": peer, "tm": t})
        copy.start()
        sent.append(copy)
    o_fin[d] = o_red[...]

    for i in range(1, N):
        slot = lax.rem(d + i, N)
        dp_arrived(g_got, slot, g1_s, g1_r, slot)
    g_red[...] = jnp.sum(g_got[...].astype(F32), axis=0).astype(BF16)
    for i in range(1, N):
        peer = lax.rem(d + i, N)
        copy = rem_copy(g_red, g_fin.at[t], g2_s.at[i], g2_r.at[t], {"dp": peer, "tm": d})
        copy.start()
        sent.append(copy)
    last = rem_copy(g_red, g_fin.at[t], g2_s.at[0], g2_r.at[t], {"dp": d, "tm": d})

    @pl.when(t != d)
    def _():
        last.start()

    @pl.when(t == d)
    def _():
        g_fin[t] = g_red[...]

    for i in range(1, N):
        dp_arrived(t_got, lax.rem(d + N - i, N), t1_s, t1_r, i)
        dp_arrived(o_fin, lax.rem(d + N - i, N), o2_s, o2_r, i)
    taps_out[...] = jnp.sum(t_got[...].astype(F32), axis=0)
    for j in range(4):
        out_out[:, j * 4 * HD : (j + 1) * 4 * HD] = jnp.concatenate(
            [o_fin[4 * j + k] for k in range(4)], axis=1
        )

    for i in range(1, N):
        slot = lax.rem(t + i, N)
        dp_arrived(g_fin, slot, g2_s, g2_r, slot)

    @pl.when(t != d)
    def _():
        dp_arrived(g_fin, t, g2_s, g2_r, t)
        last.wait_send()

    for j in range(4):
        first, second = [], []
        for k in range(4):
            s = 4 * j + k
            wide = g_fin[s, 0:HD, :]
            tail = g_fin[s, HD : HD + HD // 2, :]
            first.append(wide[:, 0:HD])
            second.append(wide[:, HD:])
            second.append(jnp.concatenate([tail[:, 0:64], tail[:, 64:]], axis=0))
        cols = slice(j * 4 * HD, (j + 1) * 4 * HD)
        glu_out[:, cols] = jnp.concatenate(first, axis=1)
        cols = slice(width + j * 4 * HD, width + (j + 1) * 4 * HD)
        glu_out[:, cols] = jnp.concatenate(second, axis=1)

    for copy in sent:
        copy.wait_send()
    for i in range(1, N):
        owner = lax.rem(d + i, N)
        rem_copy(g_own.at[owner], g_got.at[d], g1_s.at[owner], g1_r.at[d], here).wait_send()
    cot.sent()
    ug.sent()


def vmem():
    return pl.BlockSpec(memory_space=pltpu.VMEM)


def core(query, keys, values, frames, w_glu, w_out, cot, taps, norm_gain, conv_gain):
    rows, width = query.shape
    length = rows * N
    kernel = taps.shape[0]
    lanes = 128
    packed = HD + HD // 2
    dma = pltpu.SemaphoreType.DMA
    V = pltpu.VMEM
    return pl.pallas_call(
        core_kernel,
        out_shape=(
            jax.ShapeDtypeStruct((HD, 2 * width), BF16),
            jax.ShapeDtypeStruct((HD, width), BF16),
            jax.ShapeDtypeStruct((kernel, lanes), F32),
        ),
        in_specs=[vmem()] * 10,
        out_specs=(vmem(), vmem(), vmem()),
        scratch_shapes=[
            V((N, 2 * HD, rows), BF16),
            V((N, 2 * HD, rows), BF16),
            V((N, 2 * HD, rows), BF16),
            V((N, 2 * HD, rows), BF16),
            V((length, HD), BF16),
            V((HD, length), BF16),
            V((HD, length), F32),
            V((N, 2, length), F32),
            V((N, 2, length), F32),
            V((N, 2, length), F32),
            V((N, HD, 2 * HD), BF16),
            V((N, HD, 2 * HD), BF16),
            V((N, HD, length), BF16),
            V((N, rows, width), BF16),
            V((width, 128), F32),
            V((kernel, lanes), F32),
            V((2 * HD, length), F32),
            V((HD, length), F32),
            V((length + kernel, lanes), F32),
            V((length + kernel, lanes), F32),
            V((HD, length), F32),
            V((HD, length), F32),
            V((HD, length), BF16),
            V((2 * HD, length), BF16),
            V((kernel, lanes), F32),
            V((N, packed, 128), BF16),
            V((N, HD, HD), BF16),
            V((N, packed, 128), BF16),
            V((N, HD, HD), BF16),
            V((N, kernel, lanes), BF16),
            V((packed, 128), BF16),
            V((HD, HD), BF16),
            V((N, packed, 128), BF16),
            V((N, HD, HD), BF16),
        ]
        + [dma((N,))] * 12
        + [dma((15,))] * 4
        + [dma((N,))] * 10
        + [dma(())],
        compiler_params=pltpu.CompilerParams(
            collective_id=0, has_side_effects=True, vmem_limit_bytes=58 * 2**20
        ),
        name="core",
    )(query, keys, values, frames, w_glu, w_out, cot, taps, norm_gain, conv_gain)


def local(frames, query, keys, values, norm_gain, conv_gain, w_glu, taps, w_out, cotangent):
    glu_grad, out_grad, taps_grad = core(
        query[0], keys[0], values[0], frames[0], w_glu, w_out, cotangent[0], taps,
        norm_gain.reshape(1, -1), conv_gain.reshape(1, -1),
    )
    return glu_grad.astype(F32), taps_grad[:, :HD], out_grad.astype(F32)


def solution(mesh):
    return jax.shard_map(
        local,
        mesh=mesh,
        in_specs=(
            P("dp", "tm", None),
            P("dp", "tm", None),
            P("dp", "tm", None),
            P("dp", "tm", None),
            P(),
            P(),
            P("tm", None),
            P(),
            P("tm", None),
            P("dp", "tm", None),
        ),
        out_specs=(P("tm", None), P(None, "tm"), P("tm", None)),
        check_vma=False,
    )
```

time: 286 us -> 228 us (0.80); the launches traced: 281 us -> 228 us
  Pallas kernels: 245 us -> 221 us
  matrix products: 15.6 us -> 0 us
  local copies, waits for them, and re-layouts: 17.5 us -> 3.2 us
    pallas_call x3 -> x1, Pallas kernels: 245 us -> 221 us  [core(): pl.pallas_call(core_kernel, out_shape=(jax.ShapeDtypeStruct((HD, 2 * widt...]
    dot_general x4 -> x0, matrix products: 15.6 us -> none  [the longest x1 5.83 us: local(): lax.dot_general(w_out, cot_rows, (((1,), (1,)), ((), ())), preferred_elem...]
    convert_element_type x6 -> x0, local copies, waits for them, and re-layouts: 8.01 us -> none  [the longest x3 5.26 us: local(): g_all.reshape(N, HD, 2, HD).transpose(1, 2, 0, 3).reshape(HD, 2 * width)]
    reshape x8 -> x2, local copies, waits for them, and re-layouts: 7.42 us -> 2.59 us  [the longest x1 1.3 us: local(): norm_gain.reshape(1, -1)]
where the time goes in v2:
time: 228 us
  Pallas kernels  221 us (97%)
  local copies, waits for them, and re-layouts  3.2 us (1%)
  other arithmetic  3.09 us (1%)
    pallas_call x1, Pallas kernels, core(): pl.pallas_call(core_kernel, out_shape=(jax.ShapeDtypeStruct((HD, 2 * widt...  221 us

profile of v2, /device:TPU:1, one launch (start us, length us, event | category | flops | bytes accessed | tf_op | source)
XLA Modules:
  0.0 227.8 jit_solution(17434966622929264997)
XLA Ops:
  0.6 1.3 reshape.12.ng_ref
  1.9 1.3 reshape.13.cg_ref
  3.2 220.9 %core.1 = (bf16[96,3072]{1,0:T(8,128)(2,1)}, bf16[96,1536]{1,0:T(8,128)(2,1)}, f32[32,128]{1,0:T(8,128)}) custom-call(bf16[128,1536]{1,0:T(8,128)(2,1)} %bitcast.6, bf16[128,1536]{1,0:T(8,128)(2,1)} %bitcast.7, bf16[128,1536]{1,0:T(8,128)(2,1)} %bitcast.8, bf16[128,1536]{1,0:T(8,128)(2,1)} %bitcast.9, bf16[96,3072]{1,0:T(8,128)(2,1)} %wg_ref.1, ...), custom_call_target="tpu_custom_call" | custom-call | tf_op jit(solution)/shard_map/core/pallas_call | solution.py:529
  224.1 0.0 copy-start
  224.1 0.0 copy-start.1
  224.2 2.2 convert_element_type.6
  226.4 0.0 copy-done
  226.4 0.9 convert_element_type.7
  227.2 0.0 copy-done.1
  227.2 0.6 copy.14
Async XLA Ops:
  224.1 2.2 copy-start
  224.1 3.1 %copy-start.1 = (f32[32,128]{1,0:T(8,128)S(1)}, f32[32,128]{1,0:T(8,128)}, u32[]{:S(2)}) copy-start(f32[32,128]{1,0:T(8,128)} %get-tuple-element.7) | copy-start | bytes 49156

commit v3 on v2

--- a/solution.py
+++ b/solution.py
@@ -55,11 +55,17 @@
         ref = self.out.at[self.slot(block)]
         rem_copy(ref, ref, self.send.at[sem], self.recv.at[sem], {"tm": self.sib}).wait_recv()
 
-    def start(self):
+    def start_far(self):
         self.go(self.own, self.me, 0, self.far)
+
+    def start_near(self):
         for j in (0, 2, 1):
             self.go(self.own, self.me, 1 + j, self.to[j])
         self.go(self.own, self.me, 7, self.sib)
+
+    def start(self):
+        self.start_far()
+        self.start_near()
 
     def relay_far(self):
         self.landed(self.far, 0)
@@ -137,7 +143,7 @@
     w_own, w_got, u_all, cot_all, small, taps_own, p, ds, y_pad, dz_pad, z_cols, g_cols, s_cols, dp,
     t_own, g_own, o_own, g_got, o_got, t_got, g_red, o_red, g_fin, o_fin,
     kv_s, kv_r, qf_s, qf_r, w_s, w_r, st_s, st_r, sz_s, sz_r, se_s, se_r,
-    c_s, c_r, u_s, u_r, g1_s, g1_r, o1_s, o1_r, t1_s, t1_r, g2_s, g2_r, o2_s, o2_r, own_sem,
+    c_s, c_r, u_s, u_r, g1_s, g1_r, o1_s, o1_r, t1_s, t1_r, g2_s, g2_r, o2_s, o2_r, wx_s, wx_r, own_sem,
 ):
     d = lax.axis_index("dp")
     t = lax.axis_index("tm")
@@ -194,6 +200,8 @@
     turn_into(q_ref, qf_own, 0)
     turn_into(f_ref, qf_own, 1)
     scatter(qf_own, qf, t, qf_s, qf_r)
+    cot = Gather(t, cot_ref, cot_all, lambda block: block, c_s, c_r)
+    cot.start_near()
     width = N * HD
     for j in range(N):
         w_own[j] = jnp.concatenate(
@@ -203,17 +211,30 @@
             ],
             axis=1,
         )
-    scatter(w_own, w_got, place(t), w_s, w_r)
+    x_at = d // 4
+    for i in range(1, N):
+        peer = lax.rem(t + i, N)
+
+        @pl.when(x_at == y_at)
+        def _():
+            rem_copy(
+                w_own.at[peer], w_got.at[y_at, group], w_s.at[i], w_r.at[group], {"tm": peer}
+            ).start()
+
     kv[t] = kv_own[t]
     qf[t] = qf_own[t]
-    w_got[place(t)] = w_own[t]
+
+    @pl.when(x_at == y_at)
+    def _():
+        w_got[y_at, group] = w_own[t]
+
 
     small[...] = jnp.transpose(
         jnp.concatenate(
             [
                 taps_ref[...],
-                ng_ref[...],
-                cg_ref[...],
+                ng_ref[...].reshape(1, width),
+                cg_ref[...].reshape(1, width),
                 jnp.zeros((128 - kernel - 2, width), F32),
             ],
             axis=0,
@@ -235,8 +256,7 @@
     for s in range(N):
         k_rows[s * rows : (s + 1) * rows, :] = jnp.transpose(kv[s, 0:HD, :])
         v_cols[:, s * rows : (s + 1) * rows] = kv[s, HD : 2 * HD, :]
-    cot = Gather(t, cot_ref, cot_all, lambda block: block, c_s, c_r)
-    cot.start()
+    cot.start_far()
 
     factor = HD ** -0.5 * 1.4426950408889634
     pair = 2
@@ -267,6 +287,20 @@
 
     swap = Swap(t, stats, st_s, st_r)
     swap.start()
+    for g in range(4):
+
+        @pl.when(x_at * 4 + g != t)
+        def _():
+            ref = w_got.at[x_at, g]
+            rem_copy(ref, ref, w_s.at[0], w_r.at[g], {"tm": t}).wait_recv()
+
+    for i in range(1, 4):
+        ref = w_got.at[x_at]
+        copy = rem_copy(
+            ref, ref, wx_s.at[i], wx_r.at[i], {"dp": lax.rem(d + 4 * i, N), "tm": t}
+        )
+        copy.start()
+        sent.append(copy)
     cot.relay_near()
     swap.finish()
     mean, inv = joined_stats(stats)
@@ -288,12 +322,13 @@
     cot_keep.wait()
     back_rows(z_at)
 
-    for i in range(1, N):
-        arrived(w_got, place(lax.rem(t + N - i, N)), i, w_s, w_r)
+    for i in range(1, 4):
+        ref = w_got.at[lax.rem(x_at + 4 - i, 4)]
+        rem_copy(ref, ref, wx_s.at[i], wx_r.at[i], {"tm": t}).wait_recv()
     chunk = 512
 
     def product(g, first):
-        weights = w_got[pl.ds(g * 4, 4)].reshape(4 * HD, 2 * HD)
+        weights = w_got[:, pl.ds(g, 1)].reshape(4 * HD, 2 * HD)
 
         @pl.loop(0, length // chunk)
         def _(i):
@@ -388,8 +423,6 @@
             jnp.concatenate([g_cols[:, cols], blank], axis=0)
         )
 
-    t_own[...] = jnp.zeros_like(t_own)
-
     @pl.loop(0, blocks)
     def back(i):
         start = pl.multiple_of(i * step, step)
@@ -402,10 +435,6 @@
         sig = jax.nn.sigmoid(p[HD : 2 * HD, cols])
         dp[0:HD, cols] = (dy * sig).astype(BF16)
         dp[HD : 2 * HD, cols] = (dy * pa * sig * (1.0 - sig)).astype(BF16)
-        dz = dz_pad[pl.ds(pl.multiple_of(half + start, half), step), :]
-        for k in range(kernel):
-            prod = dz * y_pad[pl.ds(start + k, step), :]
-            t_own[k : k + 1, :] += jnp.sum(prod, axis=0, keepdims=True)
 
     @pl.loop(0, 4)
     def grads(i):
@@ -431,6 +460,16 @@
                 ).start()
 
     g_got[d] = g_own[d]
+    t_own[...] = jnp.zeros_like(t_own)
+
+    @pl.loop(0, blocks)
+    def tap_grads(i):
+        start = pl.multiple_of(i * step, step)
+        dz = dz_pad[pl.ds(pl.multiple_of(half + start, half), step), :]
+        for k in range(kernel):
+            prod = dz * y_pad[pl.ds(start + k, step), :]
+            t_own[k : k + 1, :] += jnp.sum(prod, axis=0, keepdims=True)
+
     t_got[d] = t_own[...].astype(BF16)
     for i in range(1, N):
         peer = lax.rem(d + i, N)
@@ -507,6 +546,13 @@
 
     for copy in sent:
         copy.wait_send()
+    for i in range(1, N):
+
+        @pl.when(x_at == y_at)
+        def _():
+            ref = w_own.at[lax.rem(t + i, N)]
+            rem_copy(ref, ref, w_s.at[i], w_r.at[group], {"tm": t}).wait_send()
+
     for i in range(1, N):
         owner = lax.rem(d + i, N)
         rem_copy(g_own.at[owner], g_got.at[d], g1_s.at[owner], g1_r.at[d], here).wait_send()
@@ -547,7 +593,7 @@
             V((N, 2, length), F32),
             V((N, 2, length), F32),
             V((N, HD, 2 * HD), BF16),
-            V((N, HD, 2 * HD), BF16),
+            V((4, 4, HD, 2 * HD), BF16),
             V((N, HD, length), BF16),
             V((N, rows, width), BF16),
             V((width, 128), F32),
@@ -574,6 +620,7 @@
         + [dma((N,))] * 12
         + [dma((15,))] * 4
         + [dma((N,))] * 10
+        + [dma((4,))] * 2
         + [dma(())],
         compiler_params=pltpu.CompilerParams(
             collective_id=0, has_side_effects=True, vmem_limit_bytes=58 * 2**20
@@ -585,7 +632,7 @@
 def local(frames, query, keys, values, norm_gain, conv_gain, w_glu, taps, w_out, cotangent):
     glu_grad, out_grad, taps_grad = core(
         query[0], keys[0], values[0], frames[0], w_glu, w_out, cotangent[0], taps,
-        norm_gain.reshape(1, -1), conv_gain.reshape(1, -1),
+        norm_gain, conv_gain,
     )
     return glu_grad.astype(F32), taps_grad[:, :HD], out_grad.astype(F32)
 

time: 228 us -> 219 us (0.961)
  Pallas kernels: 221 us -> 214 us
  local copies, waits for them, and re-layouts: 3.2 us -> 0.61 us
    pallas_call x1, Pallas kernels: 221 us -> 214 us  [core(): pl.pallas_call(core_kernel, out_shape=(jax.ShapeDtypeStruct((HD, 2 * widt...]
    reshape x2 -> x0, local copies, waits for them, and re-layouts: 2.59 us -> none  [the longest x1 1.3 us: local(): norm_gain.reshape(1, -1)]
where the time goes in v3:
time: 219 us
  Pallas kernels  214 us (98%)
  other arithmetic  3.09 us (1%)
    pallas_call x1, Pallas kernels, core(): pl.pallas_call(core_kernel, out_shape=(jax.ShapeDtypeStruct((HD, 2 * widt...  214 us

profile of v3, /device:TPU:1, one launch (start us, length us, event | category | flops | bytes accessed | tf_op | source)
XLA Modules:
  0.0 218.7 jit_solution(18150603893671408469)
XLA Ops:
  0.6 214.3 %core.1 = (bf16[96,3072]{1,0:T(8,128)(2,1)}, bf16[96,1536]{1,0:T(8,128)(2,1)}, f32[32,128]{1,0:T(8,128)}) custom-call(bf16[128,1536]{1,0:T(8,128)(2,1)} %bitcast.6, bf16[128,1536]{1,0:T(8,128)(2,1)} %bitcast.7, bf16[128,1536]{1,0:T(8,128)(2,1)} %bitcast.8, bf16[128,1536]{1,0:T(8,128)(2,1)} %bitcast.9, bf16[96,3072]{1,0:T(8,128)(2,1)} %wg_ref.1, ...), custom_call_target="tpu_custom_call" | custom-call | tf_op jit(solution)/shard_map/core/pallas_call | solution.py:575
  214.9 0.0 copy-start
  215.0 0.0 copy-start.1
  215.0 2.2 %convert_element_type.6 = f32[96,3072]{1,0:T(8,128)} convert(bf16[96,3072]{1,0:T(8,128)(2,1)} %get-tuple-element.6) | non-fusion elementwise | flops 294912 | bytes 1769472 | tf_op jit(solution)/shard_map/convert_element_type | solution.py:637
  217.2 0.0 copy-done
  217.2 0.9 convert_element_type.7
  218.1 0.0 copy-done.1
  218.1 0.6 copy.14
Async XLA Ops:
  214.9 2.2 %copy-start = (bf16[96,1536]{1,0:T(8,128)(2,1)S(1)}, bf16[96,1536]{1,0:T(8,128)(2,1)}, u32[]{:S(2)}) copy-start(bf16[96,1536]{1,0:T(8,128)(2,1)} %get-tuple-element.8) | copy-start | bytes 884740
  215.0 3.1 %copy-start.1 = (f32[32,128]{1,0:T(8,128)S(1)}, f32[32,128]{1,0:T(8,128)}, u32[]{:S(2)}) copy-start(f32[32,128]{1,0:T(8,128)} %get-tuple-element.7) | copy-start | bytes 49156

commit v4 on v3

--- a/solution.py
+++ b/solution.py
@@ -139,11 +139,11 @@
 def core_kernel(
     q_ref, k_ref, v_ref, f_ref, wg_ref, wo_ref, cot_ref, taps_ref, ng_ref, cg_ref,
     glu_out, out_out, taps_out,
-    kv_own, qf_own, kv, qf, k_rows, v_cols, mixed, stats, stats_z, stats_e,
+    kv_own, qf_own, kv, qf, k_rows, v_cols, mixed, stats_a, stats_b, stats_z, stats_e,
     w_own, w_got, u_all, cot_all, small, taps_own, p, ds, y_pad, dz_pad, z_cols, g_cols, s_cols, dp,
     t_own, g_own, o_own, g_got, o_got, t_got, g_red, o_red, g_fin, o_fin,
     kv_s, kv_r, qf_s, qf_r, w_s, w_r, st_s, st_r, sz_s, sz_r, se_s, se_r,
-    c_s, c_r, u_s, u_r, g1_s, g1_r, o1_s, o1_r, t1_s, t1_r, g2_s, g2_r, o2_s, o2_r, wx_s, wx_r, own_sem,
+    sb_s, sb_r, c_s, c_r, ua_s, ua_r, ub_s, ub_r, g1_s, g1_r, o1_s, o1_r, t1_s, t1_r, g2_s, g2_r, o2_s, o2_r, wx_s, wx_r, own_sem,
 ):
     d = lax.axis_index("dp")
     t = lax.axis_index("tm")
@@ -256,37 +256,53 @@
     for s in range(N):
         k_rows[s * rows : (s + 1) * rows, :] = jnp.transpose(kv[s, 0:HD, :])
         v_cols[:, s * rows : (s + 1) * rows] = kv[s, HD : 2 * HD, :]
-    cot.start_far()
-
     factor = HD ** -0.5 * 1.4426950408889634
     pair = 2
-
-    @pl.loop(0, N // pair)
-    def attend(i):
-        for j in range(pair):
-            s = i * pair + j
-
-            @pl.when(s != t)
-            def _():
-                arrived(qf, s, lax.rem(t + N - s, N), qf_s, qf_r)
-
-        queries = jnp.concatenate([qf[i * pair + j, 0:HD, :] for j in range(pair)], axis=1)
-        field = jnp.concatenate([qf[i * pair + j, HD : 2 * HD, :] for j in range(pair)], axis=1)
-        scores = jnp.dot(k_rows[...], queries, preferred_element_type=F32)
-        top = jnp.max(scores, axis=0, keepdims=True)
-        expo = jnp.exp2(scores * factor - top * factor)
-        total = jnp.sum(expo, axis=0, keepdims=True)
-        summed = jnp.dot(v_cols[...], expo.astype(BF16), preferred_element_type=F32)
-        attention = (summed / total).astype(BF16)
-        block = field.astype(F32) + attention.astype(F32)
-        cols = pl.ds(pl.multiple_of(i * pair * rows, pair * rows), pair * rows)
-        mixed[:, cols] = block
-        mean, square = own_stats(block)
-        stats[t, 0:1, cols] = mean
-        stats[t, 1:2, cols] = square
-
-    swap = Swap(t, stats, st_s, st_r)
-    swap.start()
+    middle = length // 2
+
+    def attend(low, high, h, stats):
+        @pl.loop(low, high)
+        def _(i):
+            for j in range(pair):
+                s = i * pair + j
+
+                @pl.when(s != t)
+                def _():
+                    arrived(qf, s, lax.rem(t + N - s, N), qf_s, qf_r)
+
+            queries = jnp.concatenate([qf[i * pair + j, 0:HD, :] for j in range(pair)], axis=1)
+            field = jnp.concatenate([qf[i * pair + j, HD : 2 * HD, :] for j in range(pair)], axis=1)
+            scores = jnp.dot(k_rows[...], queries, preferred_element_type=F32)
+            top = jnp.max(scores, axis=0, keepdims=True)
+            expo = jnp.exp2(scores * factor - top * factor)
+            total = jnp.sum(expo, axis=0, keepdims=True)
+            summed = jnp.dot(v_cols[...], expo.astype(BF16), preferred_element_type=F32)
+            attention = (summed / total).astype(BF16)
+            block = field.astype(F32) + attention.astype(F32)
+            span = pair * rows
+            mixed[:, pl.ds(pl.multiple_of(i * span, span), span)] = block
+            cols = pl.ds(pl.multiple_of((i - h * (middle // span)) * span, span), span)
+            mean, square = own_stats(block)
+            stats[t, 0:1, cols] = mean
+            stats[t, 1:2, cols] = square
+
+    def make_u(h, stats, send, recv):
+        mean, inv = joined_stats(stats)
+        v = mixed[:, h * middle : (h + 1) * middle]
+        u_all[h, place(t)] = ((v - mean) * inv * norm_gain).astype(BF16)
+        gather = Gather(t, u_all.at[h, place(t)], u_all.at[h], place, send, recv)
+        gather.start()
+        return gather
+
+    attend(0, 4, 0, stats_a)
+    swap_a = Swap(t, stats_a, st_s, st_r)
+    swap_a.start()
+    attend(4, 6, 1, stats_b)
+    swap_a.finish()
+    ua = make_u(0, stats_a, ua_s, ua_r)
+    attend(6, 8, 1, stats_b)
+    swap_b = Swap(t, stats_b, sb_s, sb_r)
+    swap_b.start()
     for g in range(4):
 
         @pl.when(x_at * 4 + g != t)
@@ -301,12 +317,12 @@
         )
         copy.start()
         sent.append(copy)
+    swap_b.finish()
+    ub = make_u(1, stats_b, ub_s, ub_r)
+    ua.relay_far()
+    ua.relay_near()
+    cot.start_far()
     cot.relay_near()
-    swap.finish()
-    mean, inv = joined_stats(stats)
-    u_all[place(t)] = ((mixed[...] - mean) * inv * norm_gain).astype(BF16)
-    ug = Gather(t, u_all.at[place(t)], u_all, place, u_s, u_r)
-    ug.start()
 
     def back_rows(z):
         @pl.loop(0, 4)
@@ -318,64 +334,77 @@
             )
 
     z_at = lax.rem(t // 2, 2)
-    cot.near_from_sibling()
-    cot_keep.wait()
-    back_rows(z_at)
-
     for i in range(1, 4):
         ref = w_got.at[lax.rem(x_at + 4 - i, 4)]
         rem_copy(ref, ref, wx_s.at[i], wx_r.at[i], {"tm": t}).wait_recv()
     chunk = 512
 
-    def product(g, first):
+    def product(g, h, first):
         weights = w_got[:, pl.ds(g, 1)].reshape(4 * HD, 2 * HD)
 
-        @pl.loop(0, length // chunk)
+        @pl.loop(0, middle // chunk)
         def _(i):
             cols = pl.ds(pl.multiple_of(i * chunk, chunk), chunk)
-            part = u_all[pl.ds(g * 4, 4), :, cols].reshape(4 * HD, chunk)
+            part = u_all[h, pl.ds(g * 4, 4), :, cols].reshape(4 * HD, chunk)
             part = lax.dot_general(
                 weights, part, (((0,), (0,)), ((), ())), preferred_element_type=F32
             )
+            cols = pl.ds(pl.multiple_of(h * middle + i * chunk, chunk), chunk)
             p[:, cols] = part if first else p[:, cols] + part
-
-    side = lax.rem(group + 1, 2) - lax.rem(group, 2)
-    ug.relay_far()
-    ug.relay_near()
-    product(group, True)
-    ug.near_from_sibling()
-    product(group + side, False)
-    ug.relay_rest()
-    cot.relay_far()
-    other = lax.rem(group + 2, 4)
-    product(other, False)
-    ug.rest_from_sibling()
-    product(other + side, False)
 
     step = 128
     blocks = length // step
 
-    @pl.loop(0, blocks)
-    def gate(i):
-        cols = pl.ds(pl.multiple_of(i * step, step), step)
-        y = p[0:HD, cols] * jax.nn.sigmoid(p[HD : 2 * HD, cols])
-        y = y.astype(BF16).astype(F32)
-        y_pad[pl.ds(pl.multiple_of(half + i * step, half), step), :] = jnp.transpose(
-            jnp.concatenate([y, blank], axis=0)
-        )
-
-    @pl.loop(0, blocks)
-    def conv(i):
-        start = pl.multiple_of(i * step, step)
-        z = jnp.zeros((step, lanes), F32)
-        for k in range(kernel):
-            z = z + taps_own[k : k + 1, :] * y_pad[pl.ds(start + k, step), :]
-        z = jnp.transpose(z)[0:HD]
-        cols = pl.ds(start, step)
-        z_cols[:, cols] = z
-        mean, square = own_stats(z)
-        stats_z[t, 0:1, cols] = mean
-        stats_z[t, 1:2, cols] = square
+    def gate(low, high):
+        @pl.loop(low, high)
+        def _(i):
+            cols = pl.ds(pl.multiple_of(i * step, step), step)
+            y = p[0:HD, cols] * jax.nn.sigmoid(p[HD : 2 * HD, cols])
+            y = y.astype(BF16).astype(F32)
+            y_pad[pl.ds(pl.multiple_of(half + i * step, half), step), :] = jnp.transpose(
+                jnp.concatenate([y, blank], axis=0)
+            )
+
+    def conv(low, high):
+        @pl.loop(low, high)
+        def _(i):
+            start = pl.multiple_of(i * step, step)
+            z = jnp.zeros((step, lanes), F32)
+            for k in range(kernel):
+                z = z + taps_own[k : k + 1, :] * y_pad[pl.ds(start + k, step), :]
+            z = jnp.transpose(z)[0:HD]
+            cols = pl.ds(start, step)
+            z_cols[:, cols] = z
+            mean, square = own_stats(z)
+            stats_z[t, 0:1, cols] = mean
+            stats_z[t, 1:2, cols] = square
+
+    side = lax.rem(group + 1, 2) - lax.rem(group, 2)
+    other = lax.rem(group + 2, 4)
+    product(group, 0, True)
+    ua.near_from_sibling()
+    product(group + side, 0, False)
+    ub.relay_far()
+    ub.relay_near()
+    ua.relay_rest()
+    cot.relay_far()
+    cot.near_from_sibling()
+    cot_keep.wait()
+    back_rows(z_at)
+    product(other, 0, False)
+    ua.rest_from_sibling()
+    product(other + side, 0, False)
+    gate(0, blocks // 2)
+    product(group, 1, True)
+    ub.near_from_sibling()
+    product(group + side, 1, False)
+    conv(0, blocks // 2 - 1)
+    ub.relay_rest()
+    product(other, 1, False)
+    ub.rest_from_sibling()
+    product(other + side, 1, False)
+    gate(blocks // 2, blocks)
+    conv(blocks // 2 - 1, blocks)
 
     swap = Swap(t, stats_z, sz_s, sz_r)
     swap.start()
@@ -439,12 +468,16 @@
     @pl.loop(0, 4)
     def grads(i):
         g = lax.rem(i + d, 4)
-        part = lax.dot_general(
-            u_all[pl.ds(g * 4, 4)].reshape(4 * HD, length),
-            dp[...],
-            (((1,), (1,)), ((), ())),
-            preferred_element_type=F32,
-        ).astype(BF16)
+        part = [
+            lax.dot_general(
+                u_all[h, pl.ds(g * 4, 4)].reshape(4 * HD, middle),
+                dp[:, h * middle : (h + 1) * middle],
+                (((1,), (1,)), ((), ())),
+                preferred_element_type=F32,
+            )
+            for h in range(2)
+        ]
+        part = (part[0] + part[1]).astype(BF16)
         for j in range(4):
             block = part[j * HD : (j + 1) * HD]
             owner = 4 * j + g
@@ -484,6 +517,25 @@
         rem_copy(ref, ref, send.at[i], recv.at[i], here).wait_recv()
 
     for i in range(1, N):
+        slot = lax.rem(d + i, N)
+        dp_arrived(g_got, slot, g1_s, g1_r, slot)
+    g_red[...] = jnp.sum(g_got[...].astype(F32), axis=0).astype(BF16)
+    for i in range(1, N):
+        peer = lax.rem(d + i, N)
+        copy = rem_copy(g_red, g_fin.at[t], g2_s.at[i], g2_r.at[t], {"dp": peer, "tm": d})
+        copy.start()
+        sent.append(copy)
+    last = rem_copy(g_red, g_fin.at[t], g2_s.at[0], g2_r.at[t], {"dp": d, "tm": d})
+
+    @pl.when(t != d)
+    def _():
+        last.start()
+
+    @pl.when(t == d)
+    def _():
+        g_fin[t] = g_red[...]
+
+    for i in range(1, N):
         dp_arrived(o_got, lax.rem(d + N - i, N), o1_s, o1_r, i)
     o_red[...] = jnp.sum(o_got[...].astype(F32), axis=0).astype(BF16)
     for i in range(1, N):
@@ -492,25 +544,6 @@
         copy.start()
         sent.append(copy)
     o_fin[d] = o_red[...]
-
-    for i in range(1, N):
-        slot = lax.rem(d + i, N)
-        dp_arrived(g_got, slot, g1_s, g1_r, slot)
-    g_red[...] = jnp.sum(g_got[...].astype(F32), axis=0).astype(BF16)
-    for i in range(1, N):
-        peer = lax.rem(d + i, N)
-        copy = rem_copy(g_red, g_fin.at[t], g2_s.at[i], g2_r.at[t], {"dp": peer, "tm": d})
-        copy.start()
-        sent.append(copy)
-    last = rem_copy(g_red, g_fin.at[t], g2_s.at[0], g2_r.at[t], {"dp": d, "tm": d})
-
-    @pl.when(t != d)
-    def _():
-        last.start()
-
-    @pl.when(t == d)
-    def _():
-        g_fin[t] = g_red[...]
 
     for i in range(1, N):
         dp_arrived(t_got, lax.rem(d + N - i, N), t1_s, t1_r, i)
@@ -557,7 +590,8 @@
         owner = lax.rem(d + i, N)
         rem_copy(g_own.at[owner], g_got.at[d], g1_s.at[owner], g1_r.at[d], here).wait_send()
     cot.sent()
-    ug.sent()
+    ua.sent()
+    ub.sent()
 
 
 def vmem():
@@ -589,12 +623,13 @@
             V((length, HD), BF16),
             V((HD, length), BF16),
             V((HD, length), F32),
-            V((N, 2, length), F32),
+            V((N, 2, length // 2), F32),
+            V((N, 2, length // 2), F32),
             V((N, 2, length), F32),
             V((N, 2, length), F32),
             V((N, HD, 2 * HD), BF16),
             V((4, 4, HD, 2 * HD), BF16),
-            V((N, HD, length), BF16),
+            V((2, N, HD, length // 2), BF16),
             V((N, rows, width), BF16),
             V((width, 128), F32),
             V((kernel, lanes), F32),
@@ -617,8 +652,8 @@
             V((N, packed, 128), BF16),
             V((N, HD, HD), BF16),
         ]
-        + [dma((N,))] * 12
-        + [dma((15,))] * 4
+        + [dma((N,))] * 14
+        + [dma((15,))] * 6
         + [dma((N,))] * 10
         + [dma((4,))] * 2
         + [dma(())],

time: 219 us -> 203 us (0.927)
  Pallas kernels: 214 us -> 197 us
    pallas_call x1, Pallas kernels: 214 us -> 197 us  [core(): pl.pallas_call(core_kernel, out_shape=(jax.ShapeDtypeStruct((HD, 2 * widt...]
where the time goes in v4:
time: 203 us; the launch traced here: 201 us
  Pallas kernels  197 us (97%)
  other arithmetic  3.09 us (2%)
    pallas_call x1, Pallas kernels, core(): pl.pallas_call(core_kernel, out_shape=(jax.ShapeDtypeStruct((HD, 2 * widt...  197 us

profile of v4, /device:TPU:1, one launch (start us, length us, event | category | flops | bytes accessed | tf_op | source)
XLA Modules:
  0.0 201.0 jit_solution(15192199278376421761)
XLA Ops:
  0.6 196.7 %core.1 = (bf16[96,3072]{1,0:T(8,128)(2,1)}, bf16[96,1536]{1,0:T(8,128)(2,1)}, f32[32,128]{1,0:T(8,128)}) custom-call(bf16[128,1536]{1,0:T(8,128)(2,1)} %bitcast.6, bf16[128,1536]{1,0:T(8,128)(2,1)} %bitcast.7, bf16[128,1536]{1,0:T(8,128)(2,1)} %bitcast.8, bf16[128,1536]{1,0:T(8,128)(2,1)} %bitcast.9, bf16[96,3072]{1,0:T(8,128)(2,1)} %wg_ref.1, ...), custom_call_target="tpu_custom_call" | custom-call | tf_op jit(solution)/shard_map/core/pallas_call | solution.py:609
  197.3 0.0 copy-start
  197.3 0.0 copy-start.1
  197.4 2.2 %convert_element_type.6 = f32[96,3072]{1,0:T(8,128)} convert(bf16[96,3072]{1,0:T(8,128)(2,1)} %get-tuple-element.6) | non-fusion elementwise | flops 294912 | bytes 1769472 | tf_op jit(solution)/shard_map/convert_element_type | solution.py:672
  199.6 0.0 copy-done
  199.6 0.9 convert_element_type.7
  200.4 0.0 copy-done.1
  200.4 0.6 copy.14
Async XLA Ops:
  197.3 2.2 %copy-start = (bf16[96,1536]{1,0:T(8,128)(2,1)S(1)}, bf16[96,1536]{1,0:T(8,128)(2,1)}, u32[]{:S(2)}) copy-start(bf16[96,1536]{1,0:T(8,128)(2,1)} %get-tuple-element.8) | copy-start | bytes 884740
  197.3 3.1 %copy-start.1 = (f32[32,128]{1,0:T(8,128)S(1)}, f32[32,128]{1,0:T(8,128)}, u32[]{:S(2)}) copy-start(f32[32,128]{1,0:T(8,128)} %get-tuple-element.7) | copy-start | bytes 49156

commit v5 on v4

--- a/solution.py
+++ b/solution.py
@@ -143,7 +143,7 @@
     w_own, w_got, u_all, cot_all, small, taps_own, p, ds, y_pad, dz_pad, z_cols, g_cols, s_cols, dp,
     t_own, g_own, o_own, g_got, o_got, t_got, g_red, o_red, g_fin, o_fin,
     kv_s, kv_r, qf_s, qf_r, w_s, w_r, st_s, st_r, sz_s, sz_r, se_s, se_r,
-    sb_s, sb_r, c_s, c_r, ua_s, ua_r, ub_s, ub_r, g1_s, g1_r, o1_s, o1_r, t1_s, t1_r, g2_s, g2_r, o2_s, o2_r, wx_s, wx_r, own_sem,
+    sb_s, sb_r, c_s, c_r, ua_s, ua_r, ub_s, ub_r, g1_s, g1_r, o1_s, o1_r, t1_s, t1_r, g2_s, g2_r, o2_s, o2_r, wx_s, wx_r, g3_s, g3_r, own_sem,
 ):
     d = lax.axis_index("dp")
     t = lax.axis_index("tm")
@@ -520,20 +520,32 @@
         slot = lax.rem(d + i, N)
         dp_arrived(g_got, slot, g1_s, g1_r, slot)
     g_red[...] = jnp.sum(g_got[...].astype(F32), axis=0).astype(BF16)
-    for i in range(1, N):
-        peer = lax.rem(d + i, N)
-        copy = rem_copy(g_red, g_fin.at[t], g2_s.at[i], g2_r.at[t], {"dp": peer, "tm": d})
-        copy.start()
-        sent.append(copy)
-    last = rem_copy(g_red, g_fin.at[t], g2_s.at[0], g2_r.at[t], {"dp": d, "tm": d})
-
-    @pl.when(t != d)
-    def _():
-        last.start()
+    g_slot = g_fin.at[t]
+    for i in range(4):
+        at_dp = y_at * 4 + lax.rem(d + i, 4)
+
+        @pl.when(jnp.logical_or(t != d, at_dp != d))
+        def _():
+            rem_copy(g_red, g_slot, g2_s.at[i], g2_r.at[group], {"dp": at_dp, "tm": d}).start()
 
     @pl.when(t == d)
     def _():
         g_fin[t] = g_red[...]
+
+    for k in range(4):
+        s = x_at * 4 + k
+
+        @pl.when(jnp.logical_or(s != t, t != d))
+        def _():
+            dp_arrived(g_fin, s, g2_s, g2_r, k)
+
+    mine = g_fin.at[pl.ds(x_at * 4, 4)]
+    for i in (1, 3, 2):
+        copy = rem_copy(
+            mine, mine, g3_s.at[i], g3_r.at[i], {"dp": lax.rem(d + 4 * i, N), "tm": t}
+        )
+        copy.start()
+        sent.append(copy)
 
     for i in range(1, N):
         dp_arrived(o_got, lax.rem(d + N - i, N), o1_s, o1_r, i)
@@ -554,14 +566,9 @@
             [o_fin[4 * j + k] for k in range(4)], axis=1
         )
 
-    for i in range(1, N):
-        slot = lax.rem(t + i, N)
-        dp_arrived(g_fin, slot, g2_s, g2_r, slot)
-
-    @pl.when(t != d)
-    def _():
-        dp_arrived(g_fin, t, g2_s, g2_r, t)
-        last.wait_send()
+    for i in range(1, 4):
+        ref = g_fin.at[pl.ds(lax.rem(x_at + 4 - i, 4) * 4, 4)]
+        rem_copy(ref, ref, g3_s.at[i], g3_r.at[i], here).wait_recv()
 
     for j in range(4):
         first, second = [], []
@@ -576,6 +583,13 @@
         glu_out[:, cols] = jnp.concatenate(first, axis=1)
         cols = slice(width + j * 4 * HD, width + (j + 1) * 4 * HD)
         glu_out[:, cols] = jnp.concatenate(second, axis=1)
+
+    for i in range(4):
+        at_dp = y_at * 4 + lax.rem(d + i, 4)
+
+        @pl.when(jnp.logical_or(t != d, at_dp != d))
+        def _():
+            rem_copy(g_red, g_slot, g2_s.at[i], g2_r.at[group], here).wait_send()
 
     for copy in sent:
         copy.wait_send()
@@ -655,7 +669,7 @@
         + [dma((N,))] * 14
         + [dma((15,))] * 6
         + [dma((N,))] * 10
-        + [dma((4,))] * 2
+        + [dma((4,))] * 4
         + [dma(())],
         compiler_params=pltpu.CompilerParams(
             collective_id=0, has_side_effects=True, vmem_limit_bytes=58 * 2**20

time: 203 us -> 199 us (0.980)
  Pallas kernels: 197 us -> 194 us
    pallas_call x1, Pallas kernels: 197 us -> 194 us  [core(): pl.pallas_call(core_kernel, out_shape=(jax.ShapeDtypeStruct((HD, 2 * widt...]
where the time goes in v5:
time: 199 us
  Pallas kernels  194 us (97%)
  other arithmetic  3.09 us (2%)
    pallas_call x1, Pallas kernels, core(): pl.pallas_call(core_kernel, out_shape=(jax.ShapeDtypeStruct((HD, 2 * widt...  194 us

profile of v5, /device:TPU:1, one launch (start us, length us, event | category | flops | bytes accessed | tf_op | source)
XLA Modules:
  0.0 198.5 jit_solution(9477577103575047373)
XLA Ops:
  0.6 194.2 %core.1 = (bf16[96,3072]{1,0:T(8,128)(2,1)}, bf16[96,1536]{1,0:T(8,128)(2,1)}, f32[32,128]{1,0:T(8,128)}) custom-call(bf16[128,1536]{1,0:T(8,128)(2,1)} %bitcast.6, bf16[128,1536]{1,0:T(8,128)(2,1)} %bitcast.7, bf16[128,1536]{1,0:T(8,128)(2,1)} %bitcast.8, bf16[128,1536]{1,0:T(8,128)(2,1)} %bitcast.9, bf16[96,3072]{1,0:T(8,128)(2,1)} %wg_ref.1, ...), custom_call_target="tpu_custom_call" | custom-call | tf_op jit(solution)/shard_map/core/pallas_call | solution.py:623
  194.8 0.0 copy-start
  194.8 0.0 copy-start.1
  194.8 2.2 %convert_element_type.6 = f32[96,3072]{1,0:T(8,128)} convert(bf16[96,3072]{1,0:T(8,128)(2,1)} %get-tuple-element.6) | non-fusion elementwise | flops 294912 | bytes 1769472 | tf_op jit(solution)/shard_map/convert_element_type | solution.py:686
  197.1 0.0 copy-done
  197.1 0.9 convert_element_type.7
  197.9 0.0 copy-done.1
  197.9 0.6 copy.14
Async XLA Ops:
  194.8 2.2 %copy-start = (bf16[96,1536]{1,0:T(8,128)(2,1)S(1)}, bf16[96,1536]{1,0:T(8,128)(2,1)}, u32[]{:S(2)}) copy-start(bf16[96,1536]{1,0:T(8,128)(2,1)} %get-tuple-element.8) | copy-start | bytes 884740
  194.8 3.1 %copy-start.1 = (f32[32,128]{1,0:T(8,128)S(1)}, f32[32,128]{1,0:T(8,128)}, u32[]{:S(2)}) copy-start(f32[32,128]{1,0:T(8,128)} %get-tuple-element.7) | copy-start | bytes 49156

commit v6 on v5

--- a/solution.py
+++ b/solution.py
@@ -137,17 +137,18 @@
 
 
 def core_kernel(
-    q_ref, k_ref, v_ref, f_ref, wg_ref, wo_ref, cot_ref, taps_ref, ng_ref, cg_ref,
+    q_in, k_ref, v_ref, f_in, wg_in, wo_in, cot_ref, taps_ref, ng_ref, cg_ref,
     glu_out, out_out, taps_out,
     kv_own, qf_own, kv, qf, k_rows, v_cols, mixed, stats_a, stats_b, stats_z, stats_e,
     w_own, w_got, u_all, cot_all, small, taps_own, p, ds, y_pad, dz_pad, z_cols, g_cols, s_cols, dp,
     t_own, g_own, o_own, g_got, o_got, t_got, g_red, o_red, g_fin, o_fin,
     kv_s, kv_r, qf_s, qf_r, w_s, w_r, st_s, st_r, sz_s, sz_r, se_s, se_r,
-    sb_s, sb_r, c_s, c_r, ua_s, ua_r, ub_s, ub_r, g1_s, g1_r, o1_s, o1_r, t1_s, t1_r, g2_s, g2_r, o2_s, o2_r, wx_s, wx_r, g3_s, g3_r, own_sem,
+    sb_s, sb_r, c_s, c_r, ua_s, ua_r, ub_s, ub_r, g1_s, g1_r, o1_s, o1_r, t1_s, t1_r, g2_s, g2_r, o2_s, o2_r, wx_s, wx_r, g3_s, g3_r, load_sem, own_sem,
+    q_ref, f_ref, wg_ref, wo_ref,
 ):
     d = lax.axis_index("dp")
     t = lax.axis_index("tm")
-    rows = q_ref.shape[0]
+    rows = k_ref.shape[0]
     length = mixed.shape[1]
     kernel = taps_ref.shape[0]
     half = kernel // 2
@@ -191,12 +192,22 @@
         ref = dst.at[slot]
         rem_copy(ref, ref, send.at[i], recv.at[i], {"tm": t}).wait_recv()
 
+    loads = [
+        pltpu.make_async_copy(src, dst, load_sem.at[i])
+        for i, (src, dst) in enumerate(
+            ((q_in, q_ref), (f_in, f_ref), (wg_in, wg_ref), (wo_in, wo_ref))
+        )
+    ]
+    for load in loads:
+        load.start()
     turn_into(k_ref, kv_own, 0)
     turn_into(v_ref, kv_own, 1)
     cot_keep = pltpu.make_async_copy(cot_ref, cot_all.at[t], own_sem)
     cot_keep.start()
     pl.semaphore_wait(barrier, jnp.where(t == d, 4 * (N - 1), 4 * (N - 1) + 2))
     scatter(kv_own, kv, t, kv_s, kv_r)
+    for load in loads:
+        load.wait()
     turn_into(q_ref, qf_own, 0)
     turn_into(f_ref, qf_own, 1)
     scatter(qf_own, qf, t, qf_s, qf_r)
@@ -566,11 +577,11 @@
             [o_fin[4 * j + k] for k in range(4)], axis=1
         )
 
-    for i in range(1, 4):
-        ref = g_fin.at[pl.ds(lax.rem(x_at + 4 - i, 4) * 4, 4)]
-        rem_copy(ref, ref, g3_s.at[i], g3_r.at[i], here).wait_recv()
-
-    for j in range(4):
+    for i in (0, 1, 3, 2):
+        j = lax.rem(x_at + 4 - i, 4)
+        if i > 0:
+            ref = g_fin.at[pl.ds(j * 4, 4)]
+            rem_copy(ref, ref, g3_s.at[i], g3_r.at[i], here).wait_recv()
         first, second = [], []
         for k in range(4):
             s = 4 * j + k
@@ -579,10 +590,10 @@
             first.append(wide[:, 0:HD])
             second.append(wide[:, HD:])
             second.append(jnp.concatenate([tail[:, 0:64], tail[:, 64:]], axis=0))
-        cols = slice(j * 4 * HD, (j + 1) * 4 * HD)
-        glu_out[:, cols] = jnp.concatenate(first, axis=1)
-        cols = slice(width + j * 4 * HD, width + (j + 1) * 4 * HD)
-        glu_out[:, cols] = jnp.concatenate(second, axis=1)
+        base = pl.multiple_of(j * 4 * HD, 4 * HD)
+        glu_out[:, pl.ds(base, 4 * HD)] = jnp.concatenate(first, axis=1)
+        base = pl.multiple_of(width + j * 4 * HD, 4 * HD)
+        glu_out[:, pl.ds(base, 4 * HD)] = jnp.concatenate(second, axis=1)
 
     for i in range(4):
         at_dp = y_at * 4 + lax.rem(d + i, 4)
@@ -606,6 +617,10 @@
     cot.sent()
     ua.sent()
     ub.sent()
+
+
+def anywhere():
+    return pl.BlockSpec(memory_space=pl.ANY)
 
 
 def vmem():
@@ -627,7 +642,7 @@
             jax.ShapeDtypeStruct((HD, width), BF16),
             jax.ShapeDtypeStruct((kernel, lanes), F32),
         ),
-        in_specs=[vmem()] * 10,
+        in_specs=[anywhere(), vmem(), vmem()] + [anywhere()] * 4 + [vmem()] * 3,
         out_specs=(vmem(), vmem(), vmem()),
         scratch_shapes=[
             V((N, 2 * HD, rows), BF16),
@@ -669,8 +684,14 @@
         + [dma((N,))] * 14
         + [dma((15,))] * 6
         + [dma((N,))] * 10
-        + [dma((4,))] * 4
-        + [dma(())],
+        + [dma((4,))] * 5
+        + [dma(())]
+        + [
+            V((rows, width), BF16),
+            V((rows, width), BF16),
+            V((HD, 2 * width), BF16),
+            V((HD, width), BF16),
+        ],
         compiler_params=pltpu.CompilerParams(
             collective_id=0, has_side_effects=True, vmem_limit_bytes=58 * 2**20
         ),

time: 199 us -> 198 us (level)
  no operation moved by 1% of the time
where the time goes in v6:
time: 198 us
  Pallas kernels  194 us (98%)
  other arithmetic  3.09 us (2%)
    pallas_call x1, Pallas kernels, core(): pl.pallas_call(core_kernel, out_shape=(jax.ShapeDtypeStruct((HD, 2 * widt...  194 us

profile of v6, /device:TPU:1, one launch (start us, length us, event | category | flops | bytes accessed | tf_op | source)
XLA Modules:
  0.0 197.9 jit_solution(11752342075992647974)
XLA Ops:
  0.6 193.5 %core.1 = (bf16[96,3072]{1,0:T(8,128)(2,1)}, bf16[96,1536]{1,0:T(8,128)(2,1)}, f32[32,128]{1,0:T(8,128)}) custom-call(bf16[128,1536]{1,0:T(8,128)(2,1)} %bitcast.6, bf16[128,1536]{1,0:T(8,128)(2,1)} %bitcast.7, bf16[128,1536]{1,0:T(8,128)(2,1)} %bitcast.8, bf16[128,1536]{1,0:T(8,128)(2,1)} %bitcast.9, bf16[96,3072]{1,0:T(8,128)(2,1)} %wg_in.1, ...), custom_call_target="tpu_custom_call" | custom-call | tf_op jit(solution)/shard_map/core/pallas_call | solution.py:638
  194.2 0.0 copy-start
  194.2 0.0 copy-start.1
  194.2 2.2 %convert_element_type.6 = f32[96,3072]{1,0:T(8,128)} convert(bf16[96,3072]{1,0:T(8,128)(2,1)} %get-tuple-element.6) | non-fusion elementwise | flops 294912 | bytes 1769472 | tf_op jit(solution)/shard_map/convert_element_type | solution.py:707
  196.4 0.0 copy-done
  196.4 0.9 convert_element_type.7
  197.3 0.0 copy-done.1
  197.3 0.6 copy.14
Async XLA Ops:
  194.2 2.2 %copy-start = (bf16[96,1536]{1,0:T(8,128)(2,1)S(1)}, bf16[96,1536]{1,0:T(8,128)(2,1)}, u32[]{:S(2)}) copy-start(bf16[96,1536]{1,0:T(8,128)(2,1)} %get-tuple-element.8) | copy-start | bytes 884740
  194.2 3.1 %copy-start.1 = (f32[32,128]{1,0:T(8,128)S(1)}, f32[32,128]{1,0:T(8,128)}, u32[]{:S(2)}) copy-start(f32[32,128]{1,0:T(8,128)} %get-tuple-element.7) | copy-start | bytes 49156

commit v7 on v6

--- a/solution.py
+++ b/solution.py
@@ -102,7 +102,7 @@
         self.started = []
 
     def start(self):
-        for i in range(1, N):
+        for i in (2, 6, 10, 14, 1, 3, 5, 7, 9, 11, 13, 15, 4, 8, 12):
             copy = rem_copy(
                 self.buf.at[self.me],
                 self.buf.at[self.me],

time: 198 us -> 197 us (level)
  Pallas kernels: 194 us -> 192 us
where the time goes in v7:
time: 197 us
  Pallas kernels  192 us (97%)
  other arithmetic  3.09 us (2%)
    pallas_call x1, Pallas kernels, core(): pl.pallas_call(core_kernel, out_shape=(jax.ShapeDtypeStruct((HD, 2 * widt...  192 us

profile of v7, /device:TPU:1, one launch (start us, length us, event | category | flops | bytes accessed | tf_op | source)
XLA Modules:
  0.0 196.6 jit_solution(17405989479613147825)
XLA Ops:
  0.6 192.2 %core.1 = (bf16[96,3072]{1,0:T(8,128)(2,1)}, bf16[96,1536]{1,0:T(8,128)(2,1)}, f32[32,128]{1,0:T(8,128)}) custom-call(bf16[128,1536]{1,0:T(8,128)(2,1)} %bitcast.6, bf16[128,1536]{1,0:T(8,128)(2,1)} %bitcast.7, bf16[128,1536]{1,0:T(8,128)(2,1)} %bitcast.8, bf16[128,1536]{1,0:T(8,128)(2,1)} %bitcast.9, bf16[96,3072]{1,0:T(8,128)(2,1)} %wg_in.1, ...), custom_call_target="tpu_custom_call" | custom-call | tf_op jit(solution)/shard_map/core/pallas_call | solution.py:638
  192.9 0.0 copy-start
  192.9 0.0 copy-start.1
  192.9 2.2 %convert_element_type.6 = f32[96,3072]{1,0:T(8,128)} convert(bf16[96,3072]{1,0:T(8,128)(2,1)} %get-tuple-element.6) | non-fusion elementwise | flops 294912 | bytes 1769472 | tf_op jit(solution)/shard_map/convert_element_type | solution.py:707
  195.1 0.0 copy-done
  195.1 0.9 convert_element_type.7
  196.0 0.0 copy-done.1
  196.0 0.6 copy.14
Async XLA Ops:
  192.9 2.2 %copy-start = (bf16[96,1536]{1,0:T(8,128)(2,1)S(1)}, bf16[96,1536]{1,0:T(8,128)(2,1)}, u32[]{:S(2)}) copy-start(bf16[96,1536]{1,0:T(8,128)(2,1)} %get-tuple-element.8) | copy-start | bytes 884740
  192.9 3.1 %copy-start.1 = (f32[32,128]{1,0:T(8,128)S(1)}, f32[32,128]{1,0:T(8,128)}, u32[]{:S(2)}) copy-start(f32[32,128]{1,0:T(8,128)} %get-tuple-element.7) | copy-start | bytes 49156
